TPU v7x, 128 devices: a whole 4x4x4 slice. The times are simulated.
128 devices in a mesh: dp: 16 (over y, z_hi, core), mp: 8 (over z_lo, x).
Axes of the slice: x: 4, y: 4, z: 4 (z_hi: 2, z_lo: 2; z = z_hi * 2 + z_lo), core: 2. Of those that a mesh axis runs over, the one named last changes fastest.
Arguments:
- activations: bfloat16 [16384, 4096], P(('dp', 'mp')), may hold values from -6 to 6
- out_grad: bfloat16 [16384, 8192], P('dp', 'mp'), may hold values from -0.046875 to 0.046875
- statistics: float32 [8, 16, 2, 512, 512], P('mp', 'dp'), as said below
- root_blocks: float32 [8, 16, 2, 512, 512], P('mp', 'dp'), as said below
- owner_slots: int32 [8, 16], P('mp'), may hold values from 0 to 15, each once within a row
- stagger_phase: int32 [8], P('mp'), may hold values from 0 to 7
Outputs:
- update: bfloat16 [4096, 8192], P(None, 'mp')
- new_statistics: float32 [8, 16, 2, 512, 512], P('mp', 'dp')
- new_roots: float32 [8, 16, 2, 512, 512], P('mp', 'dp')
Inputs may be any that keep to these rules, and one draw needn't show every extreme that they name: `statistics`: each [m, s, side] matrix is symmetric positive definite. `root_blocks`: each [m, s, side] matrix is symmetric positive definite. `owner_slots`: row m gives every block of model shard m its own slot.
All inputs are finite; a program needn't handle non-finite values.
Results may differ from a plain program's by a relative error of at most 0.019.
Values may be sent and summed in bfloat16 or wider, within the bound.
No kernel may reach another device: no remote copies, remote signals or barrier semaphores. Data moves between devices by JAX's collectives and lax.ppermute only.
A program may use at most 128 MiB of HBM per device.

v0:
```python
import jax
import jax.numpy as jnp
from jax import lax
from jax.sharding import PartitionSpec as P

FEAT = 4096
BLOCK = 512
ITERS = 3
ROW_BLK = 8


def product(left_side, right_side):
    return jnp.dot(
        left_side, right_side, precision=lax.Precision.HIGHEST, preferred_element_type=jnp.float32
    )


def inverse_root(matrix):
    identity = jnp.eye(BLOCK, dtype=jnp.float32)
    scaling = 2.5 / jnp.sqrt(jnp.sum(matrix * matrix))
    iterate = identity * jnp.sqrt(jnp.sqrt(scaling))
    coupled = matrix * scaling
    for iteration in range(ITERS):
        factor = (5.0 * identity - coupled) * 0.25
        iterate = product(iterate, factor)
        square = product(factor, factor)
        fourth = product(square, square)
        coupled = product(fourth, coupled)
    return iterate


def body(activations, out_grad, statistics, root_blocks, owner_slots, stagger_phase):
    dp_count = lax.axis_size("dp")
    dp_place = lax.axis_index("dp")
    column_count = out_grad.shape[1]
    column_blocks = column_count // BLOCK
    blocks_all = ROW_BLK * column_blocks
    per_owner = blocks_all // dp_count
    slot_of = owner_slots[0]
    numbers = jnp.arange(blocks_all, dtype=jnp.int32)
    block_at = jnp.sum(jnp.where(slot_of[:, None] == numbers[None, :], numbers[:, None], 0), axis=0)
    local_grad = lax.dot_general(
        lax.all_gather(activations, "mp", axis=0, tiled=True),
        out_grad,
        (((0,), (0,)), ((), ())),
        preferred_element_type=jnp.float32,
    )
    blocks = (
        local_grad.reshape(ROW_BLK, BLOCK, column_blocks, BLOCK)
        .transpose(0, 2, 1, 3)
        .reshape(blocks_all, BLOCK, BLOCK)
    )
    slotted = jnp.take(blocks, block_at, axis=0)
    owned_sum = lax.psum_scatter(
        slotted.astype(jnp.bfloat16), "dp", scatter_dimension=0, tiled=True
    ).astype(jnp.float32)
    highest = lax.Precision.HIGHEST
    left_gram = jnp.einsum("sij,skj->sik", owned_sum, owned_sum, precision=highest)
    right_gram = jnp.einsum("sji,sjk->sik", owned_sum, owned_sum, precision=highest)
    new_statistics = 0.95 * statistics + jnp.stack([left_gram, right_gram], axis=1)[None]
    applied = jnp.einsum("sij,sjk->sik", root_blocks[0, :, 0], owned_sum, precision=highest)
    applied = jnp.einsum("sij,sjk->sik", applied, root_blocks[0, :, 1], precision=highest).astype(
        jnp.bfloat16
    )
    all_updates = lax.all_gather(applied, "dp", axis=0, tiled=True)
    ordered = jnp.take(all_updates, slot_of, axis=0)
    update = (
        ordered.reshape(ROW_BLK, column_blocks, BLOCK, BLOCK)
        .transpose(0, 2, 1, 3)
        .reshape(FEAT, column_count)
    )
    own_blocks = lax.dynamic_slice_in_dim(block_at, dp_place * per_owner, per_owner)
    refresh_flags = (own_blocks + stagger_phase[0]) % 8 == 0
    fresh_stats = new_statistics[0]

    def refresh_slot(slot_item):
        slot_flag, matrices, stale_pair = slot_item
        return lax.cond(
            slot_flag,
            lambda: jnp.stack([inverse_root(matrices[0]), inverse_root(matrices[1])]),
            lambda: stale_pair,
        )

    new_roots = lax.map(refresh_slot, (refresh_flags, fresh_stats, root_blocks[0]))
    return (update, new_statistics, new_roots[None])


def solution(mesh):
    return jax.shard_map(
        body,
        mesh=mesh,
        in_specs=(
            P(("dp", "mp"), None),
            P("dp", "mp"),
            P("mp", "dp", None, None, None),
            P("mp", "dp", None, None, None),
            P("mp", None),
            P("mp"),
        ),
        out_specs=(P(None, "mp"), P("mp", "dp", None, None, None), P("mp", "dp", None, None, None)),
        check_vma=False,
    )
```

profile of v0, /device:TPU:1, one launch (start us, length us, event | category | flops | bytes accessed | tf_op | source)
XLA Modules:
  0.0 381.2 jit_solution(3528361385867681294)
XLA Ops:
  7.2 3.2 copy.19
  10.7 95.1 %all-gather.4.cloned.1.call-done = bf16[1024,4096]{1,0:T(8,128)(2,1)} async-done(((bf16[128,4096]{1,0:T(8,128)(2,1)}), bf16[1024,4096]{1,0:T(8,128)(2,1)}) %all-gather.4.cloned.1.call-update) | async-done | bytes 8388624 | tf_op jit(solution)/shard_map/all_gather | solution.py:43
  105.8 14.6 %fusion.107 = bf16[4096,1024]{1,0:T(8,128)(2,1)} fusion(bf16[1024,4096]{1,0:T(8,128)(2,1)} %all-gather.4.cloned.1.call-done, bf16[1024,1024]{1,0:T(8,128)(2,1)S(1)} %copy-done), kind=kOutput, calls=%fused_computation.134 | convolution fusion | flops 8589934592 | bytes 18874368 | tf_op jit(solution)/shard_map/dot_general | solution.py:42
  120.4 14.5 %reshape.214 = bf16[8,512,2,512]{3,2,1,0:T(2,128)(2,1)} reshape(bf16[4096,1024]{1,0:T(8,128)(2,1)} %fusion.107) | data formatting | bytes 16777216 | tf_op jit(solution)/shard_map/reshape | solution.py:49
  134.8 8.5 %copy.12 = bf16[8,512,2,512]{3,1,2,0:T(8,128)(2,1)} copy(bf16[8,512,2,512]{3,2,1,0:T(2,128)(2,1)} %reshape.214) | data formatting | bytes 16777216 | tf_op jit(solution)/shard_map/reshape | solution.py:49
  143.3 8.1 %gather_fusion = bf16[16,512,512]{2,1,0:T(8,128)(2,1)} fusion(bf16[16,512,512]{2,1,0:T(8,128)(2,1)} %bitcast.100, s32[1024]{0:T(1024)S(1)} %pad_clamp_fusion.1), kind=kCustom, calls=%fused_computation | custom fusion | bytes 16777280 | tf_op jit(solution)/shard_map/jit(_take)/gather | solution.py:53
  151.5 8.9 %select_convert_fusion = bf16[16,512,512]{2,1,0:T(8,128)(2,1)} fusion(bf16[16,512,512]{2,1,0:T(8,128)(2,1)} %gather_fusion, pred[16]{0:T(512)(128)(4,1)S(1)} %compare_and_fusion.1), kind=kLoop, calls=%fused_computation.103 | loop fusion | flops 4194304 | bytes 16777232 | tf_op jit(solution)/shard_map/convert_element_type | solution.py:55
  160.6 100.0 %reduce-scatter.2.cloned.1.call-done = bf16[1,512,512]{2,1,0:T(8,128)(2,1)} async-done(((bf16[16,512,512]{2,1,0:T(8,128)(2,1)}), bf16[1,512,512]{2,1,0:T(8,128)(2,1)}) %reduce-scatter.2.cloned.1.call-update) | async-done | bytes 524304 | tf_op jit(solution)/shard_map/reduce_scatter | solution.py:54
  260.7 2.3 fusion.94
  262.9 2.6 convolution_convert_fusion
  272.2 47.1 %conditional.1 = (f32[1,1,2,512,512]{4,3,2,1,0:T(8,128)S(1)}) conditional(s32[]{:T(128)} %bitcast.25, f32[1,1,2,512,512]{4,3,2,1,0:T(8,128)S(1)} %copy-done.2, f32[1,1,2,512,512]{4,3,2,1,0:T(8,128)} %fusion.92), branch_computations={%region_2.3_spmd, %region_3.6_spmd} | conditional | flops 29005709312 | bytes 52428920 | solution.py:78
  272.2 2.5 multiply_reduce_fusion.1
  275.5 3.2 fusion.15
  278.7 3.6 fusion.8
  284.1 3.1 fusion.19
  291.0 2.0 fusion.106
  297.4 3.1 fusion.11
  300.6 3.6 fusion.4
  306.1 3.1 fusion.23
  309.2 2.1 fusion.34
  319.3 19.6 %all-gather.6.cloned.1.call-done = bf16[8192,512]{1,0:T(8,128)(2,1)} async-done(((bf16[512,512]{1,0:T(8,128)(2,1)}), bf16[8192,512]{1,0:T(8,128)(2,1)}) %all-gather.6.cloned.1.call-update) | async-done | bytes 8388624 | tf_op jit(solution)/shard_map/all_gather | solution.py:65
  338.8 8.3 %gather_fusion.1 = bf16[16,512,512]{2,1,0:T(8,128)(2,1)} fusion(bf16[16,512,512]{2,1,0:T(8,128)(2,1)} %bitcast.102, s32[1024]{0:T(1024)S(1)} %pad_clamp_fusion), kind=kCustom, calls=%fused_computation.1 | custom fusion | bytes 16777280 | tf_op jit(solution)/shard_map/jit(_take)/gather | solution.py:66
  347.2 17.6 %broadcast_select_fusion = bf16[8,2,512,512]{3,1,2,0:T(2,128)(2,1)} fusion(pred[8,2]{1,0:T(8,128)(4,1)S(1)} %compare_and_fusion, bf16[8,2,512,512]{3,2,1,0:T(8,128)(2,1)} %bitcast.99), kind=kLoop, calls=%fused_computation.104 | loop fusion | flops 4194304 | bytes 16777232 | tf_op jit(solution)/shard_map/jit(_take)/select_n | solution.py:66
  364.8 9.6 %copy.14 = bf16[512,8,2,512]{3,1,2,0:T(8,128)(2,1)} copy(bf16[512,8,2,512]{3,2,1,0:T(2,128)(2,1)} %bitcast.101) | data formatting | bytes 16777216
  (45 shorter events, 24.6 us)
Async XLA Ops:
  7.2 98.6 %copy-start = (bf16[1024,1024]{1,0:T(8,128)(2,1)S(1)}, bf16[1024,1024]{1,0:T(8,128)(2,1)}, u32[]{:S(2)}) copy-start(bf16[1024,1024]{1,0:T(8,128)(2,1)} %param.9) | copy-start | bytes 6291460
  7.2 3.4 copy-start.6
  7.2 98.6 %all-gather.4.cloned.1.call-start = ((), (), s32[]{:S(2)}) async-start(), calls=%async_computation.1 | async-start | bytes 9437184 | tf_op jit(solution)/shard_map/all_gather | solution.py:43
  10.5 250.2 %reduce-scatter.2.cloned.1.call-start = ((), (), s32[]{:S(2)}) async-start(), calls=%async_computation.2 | async-start | bytes 8912896 | tf_op jit(solution)/shard_map/reduce_scatter | solution.py:54
  160.4 100.3 %copy-start.2 = (f32[1,1,2,512,512]{4,3,2,1,0:T(8,128)S(1)}, f32[1,1,2,512,512]{4,3,2,1,0:T(8,128)}, u32[]{:S(2)}) copy-start(f32[1,1,2,512,512]{4,3,2,1,0:T(8,128)} %copy.19) | copy-start | bytes 6291460
  160.4 178.4 %all-gather.6.cloned.1.call-start = ((), (), s32[]{:S(2)}) async-start(), calls=%async_computation.3 | async-start | bytes 8912896 | tf_op jit(solution)/shard_map/all_gather | solution.py:65
  262.9 5.9 %copy-start.4 = (bf16[1,512,512]{2,1,0:T(8,128)(2,1)S(1)}, bf16[1,512,512]{2,1,0:T(8,128)(2,1)}, u32[]{:S(2)}) copy-start(bf16[1,512,512]{2,1,0:T(8,128)(2,1)} %reduce-scatter.2.cloned.1.call-done) | copy-start | bytes 1572868
  268.8 1.6 copy-start.5
  319.3 27.9 %copy-start.3 = (f32[1,1,2,512,512]{4,3,2,1,0:T(8,128)}, f32[1,1,2,512,512]{4,3,2,1,0:T(8,128)S(1)}, u32[]{:S(2)}) copy-start(f32[1,1,2,512,512]{4,3,2,1,0:T(8,128)S(1)} %get-tuple-element.30) | copy-start | bytes 6291460
  364.8 9.6 %copy-start.1 = (bf16[1024,1024]{1,0:T(8,128)(2,1)S(1)}, bf16[1024,1024]{1,0:T(8,128)(2,1)}, u32[]{:S(2)}) copy-start(bf16[1024,1024]{1,0:T(8,128)(2,1)} %param.9) | copy-start | bytes 6291460
Sparse Core Ops, SparseCore 0:
  10.6 95.1 all-gather.3
  160.5 100.0 reduce-scatter.1
  265.7 73.0 all-gather.5
where the time goes:
time: 389 us; the launch traced here: 381 us
  waiting for transfers between devices  215 us (55%)
  matrix products  62.9 us (16%)
  local copies, waits for them, and re-layouts  54.1 us (14%)
  other arithmetic  31.8 us (8%)
  between operations  15.4 us (4%)
    reduce_scatter x1, waiting for transfers between devices, body(): lax.psum_scatter(slotted.astype(jnp.bfloat16), 'dp', scatter_dimension=0,...  100 us
    all_gather x1, waiting for transfers between devices, body(): lax.all_gather(activations, 'mp', axis=0, tiled=True)  95.1 us
    dot_general x18, matrix products, product(): jnp.dot(left_side, right_side, precision=lax.Precision.HIGHEST, preferred...  42.5 us
    reshape x2, local copies, waits for them, and re-layouts, body(): local_grad.reshape(ROW_BLK, BLOCK, column_blocks, BLOCK)  23 us
    all_gather x1, waiting for transfers between devices, body(): all_updates = lax.all_gather(applied, 'dp', axis=0, tiled=True)  19.6 us
    select_n x2, other arithmetic, body(): ordered = jnp.take(all_updates, slot_of, axis=0)  17.6 us
    dot_general x1, matrix products, body(): lax.dot_general(lax.all_gather(activations, 'mp', axis=0, tiled=True), ou...  14.6 us
    unnamed x17, local copies, waits for them, and re-layouts  14 us
  transfers between devices with their start and end apart: 3, of which 3 were waited for; matrix products, arithmetic and copies ran while one was open for 13% of the time, Pallas kernels for 0%

commit v1 on v0

v1 whole, which is shorter than its diff:
```python
import functools

import jax
import jax.numpy as jnp
from jax import lax
from jax.experimental import pallas as pl
from jax.experimental.pallas import tpu as pltpu
from jax.sharding import PartitionSpec as P

FEAT = 4096
BLOCK = 512
ROW_BLK = 8
COL_BLK = 2
BLOCKS = ROW_BLK * COL_BLK
CHUNKS = (256, 256)
Y, ZH, CORE, ZL, X = 4, 2, 2, 2, 4
N_MP = ZL * X
MIB = 1 << 20


def device_of(y, zh, core, zl, x):
    return ((y * ZH + zh) * CORE + core) * N_MP + zl * X + x


def pairs(move):
    out = []
    for y in range(Y):
        for zh in range(ZH):
            for core in range(CORE):
                for zl in range(ZL):
                    for x in range(X):
                        here = (y, zh, core, zl, x)
                        out.append((device_of(*here), device_of(*move(*here))))
    return out


def way(core):
    return 1 if core == 0 else -1


X_NEAR = pairs(lambda y, zh, c, zl, x: (y, zh, c, zl, (x + way(c)) % X))
X_BACK = pairs(lambda y, zh, c, zl, x: (y, zh, c, zl, (x - way(c)) % X))
Y_NEAR = pairs(lambda y, zh, c, zl, x: ((y + way(c)) % Y, zh, c, zl, x))
Y_BACK = pairs(lambda y, zh, c, zl, x: ((y - way(c)) % Y, zh, c, zl, x))
Y_FAR = pairs(lambda y, zh, c, zl, x: ((y + 2) % Y, zh, c, zl, x))
ZL_SWAP = pairs(lambda y, zh, c, zl, x: (y, zh, c, 1 - zl, x))
ZH_SWAP = pairs(lambda y, zh, c, zl, x: (y, 1 - zh, c, zl, x))
C_SWAP = pairs(lambda y, zh, c, zl, x: (y, zh, 1 - c, zl, x))


def move(value, route):
    return lax.ppermute(value, ("dp", "mp"), route)


def cost(flops, moved):
    return pl.CostEstimate(flops=int(flops), bytes_accessed=int(moved), transcendentals=0)


def params(mib, grid=1):
    return pltpu.CompilerParams(
        vmem_limit_bytes=mib * MIB, dimension_semantics=("arbitrary",) * grid
    )


def mm(a, b, contract):
    return lax.dot_general(a, b, (contract, ((), ())), preferred_element_type=jnp.float32)


def split(value):
    high = value.astype(jnp.bfloat16)
    return high, (value - high.astype(jnp.float32)).astype(jnp.bfloat16)


def mm3(a, b, contract=((1,), (0,))):
    a_high, a_low = a
    b_high, b_low = b
    return (
        mm(a_high, b_high, contract) + mm(a_high, b_low, contract) + mm(a_low, b_high, contract)
    )


def grad_kernel(rows_of, dest_of, *refs):
    pieces = refs[:N_MP]
    og_ref, keep_ref, send_ref, gathered, tiles, sems = refs[N_MP:]
    row = pl.program_id(0)
    part = pieces[0].shape[0]
    for i in range(N_MP):
        gathered[pl.ds(pl.multiple_of(rows_of[i] * part, part), part), :] = pieces[i][...]
    grad = mm(gathered[...], og_ref[...], ((0,), (0,)))
    for col in range(COL_BLK):
        number = row * COL_BLK + col
        dest = dest_of[number]
        tiles[number] = grad[:, col * BLOCK : (col + 1) * BLOCK].astype(jnp.bfloat16)

        @pl.when(dest < BLOCKS // 2)
        def _():
            pltpu.make_async_copy(tiles.at[number], keep_ref.at[dest], sems.at[number]).start()

        @pl.when(dest >= BLOCKS // 2)
        def _():
            pltpu.make_async_copy(
                tiles.at[number], send_ref.at[dest - BLOCKS // 2], sems.at[number]
            ).start()

    @pl.when(row == ROW_BLK - 1)
    def _():
        for number in range(BLOCKS):
            pltpu.make_async_copy(tiles.at[number], keep_ref.at[0], sems.at[number]).wait()


def grad_chunk(pieces, rows_of, dest_of, og, rows):
    part = pieces[0].shape[0]
    tokens, cols = og.shape
    half = jax.ShapeDtypeStruct((BLOCKS // 2, rows, BLOCK), jnp.bfloat16)
    return pl.pallas_call(
        grad_kernel,
        out_shape=(half, half),
        grid_spec=pltpu.PrefetchScalarGridSpec(
            num_scalar_prefetch=2,
            grid=(ROW_BLK,),
            in_specs=[pl.BlockSpec((part, rows), lambda r, *_: (0, r))] * N_MP
            + [pl.BlockSpec((tokens, cols), lambda r, *_: (0, 0))],
            out_specs=[pl.BlockSpec(memory_space=pl.ANY)] * 2,
            scratch_shapes=[
                pltpu.VMEM((tokens, rows), jnp.bfloat16),
                pltpu.VMEM((BLOCKS, rows, BLOCK), jnp.bfloat16),
                pltpu.SemaphoreType.DMA((BLOCKS,)),
            ],
        ),
        compiler_params=params(32),
        cost_estimate=cost(2 * tokens * cols * rows * ROW_BLK, 2 * 5 * MIB),
        name="grad_chunk",
    )(rows_of, dest_of, *pieces, og)


def chip_kernel(_, *refs):
    for d in range(Y):
        total = refs[d][...].astype(jnp.float32) + refs[Y + d][...].astype(jnp.float32)
        refs[2 * Y + d][...] = total.astype(jnp.bfloat16)


def chip_sum(keep, received, groups):
    rows = keep.shape[1]
    block = (1, rows, BLOCK)
    ins = [
        pl.BlockSpec(block, functools.partial(lambda d, j, g: (g[d] * ZH + j, 0, 0), d))
        for d in range(Y)
    ]
    out = jax.ShapeDtypeStruct((ZH, rows, BLOCK), jnp.bfloat16)
    return pl.pallas_call(
        chip_kernel,
        out_shape=(out,) * Y,
        grid_spec=pltpu.PrefetchScalarGridSpec(
            num_scalar_prefetch=1,
            grid=(ZH,),
            in_specs=ins + ins,
            out_specs=[pl.BlockSpec(block, lambda j, g: (j, 0, 0))] * Y,
        ),
        compiler_params=params(16),
        cost_estimate=cost(MIB, keep.size * 6),
        name="chip_sum",
    )(groups, *[keep] * Y, *[received] * Y)


def y_kernel(_, *refs):
    mine = sum(refs[i][0].astype(jnp.float32) for i in range(Y))
    other = sum(refs[Y + i][0].astype(jnp.float32) for i in range(Y))
    refs[2 * Y][...] = mine
    refs[2 * Y + 1][...] = other.astype(jnp.bfloat16)


def y_sum(parts, zh):
    rows = parts[0].shape[1]
    tile = min(rows, 128)
    mine = pl.BlockSpec((1, tile, BLOCK), lambda j, z: (z[0], j, 0))
    other = pl.BlockSpec((1, tile, BLOCK), lambda j, z: (1 - z[0], j, 0))
    out = pl.BlockSpec((tile, BLOCK), lambda j, z: (j, 0))
    return pl.pallas_call(
        y_kernel,
        out_shape=(
            jax.ShapeDtypeStruct((rows, BLOCK), jnp.float32),
            jax.ShapeDtypeStruct((rows, BLOCK), jnp.bfloat16),
        ),
        grid_spec=pltpu.PrefetchScalarGridSpec(
            num_scalar_prefetch=1,
            grid=(rows // tile,),
            in_specs=[mine] * Y + [other] * Y,
            out_specs=[out, out],
        ),
        compiler_params=params(16),
        cost_estimate=cost(MIB, rows * BLOCK * 22),
        name="y_sum",
    )(zh, *parts, *parts)


def apply_kernel(*refs):
    count = len(CHUNKS)
    roots_ref, update_ref, grad_ref = refs[2 * count :]
    at = 0
    for i, rows in enumerate(CHUNKS):
        grad_ref[at : at + rows] = refs[i][...] + refs[count + i][...].astype(jnp.float32)
        at += rows
    grad = split(grad_ref[...])
    right = mm3(grad, split(roots_ref[1]))
    update_ref[...] = mm3(split(roots_ref[0]), split(right)).astype(jnp.bfloat16)


def apply_roots(kept, received, roots):
    whole = pl.BlockSpec(memory_space=pltpu.VMEM)
    return pl.pallas_call(
        apply_kernel,
        out_shape=(
            jax.ShapeDtypeStruct((BLOCK, BLOCK), jnp.bfloat16),
            jax.ShapeDtypeStruct((BLOCK, BLOCK), jnp.float32),
        ),
        in_specs=[whole] * (2 * len(CHUNKS) + 1),
        out_specs=(whole, whole),
        compiler_params=pltpu.CompilerParams(vmem_limit_bytes=24 * MIB),
        cost_estimate=cost(6 * 2 * BLOCK**3, 5 * MIB),
        name="apply_roots",
    )(*kept, *received, roots)


def stats_kernel(grad_ref, stats_ref, out_ref):
    grad = split(grad_ref[...])
    out_ref[0] = 0.95 * stats_ref[0] + mm3(grad, grad, ((1,), (1,)))
    out_ref[1] = 0.95 * stats_ref[1] + mm3(grad, grad, ((0,), (0,)))


def statistics_of(grad, stats):
    whole = pl.BlockSpec(memory_space=pltpu.VMEM)
    return pl.pallas_call(
        stats_kernel,
        out_shape=jax.ShapeDtypeStruct(stats.shape, jnp.float32),
        in_specs=[whole] * 2,
        out_specs=whole,
        compiler_params=pltpu.CompilerParams(vmem_limit_bytes=24 * MIB),
        cost_estimate=cost(6 * 2 * BLOCK**3, 5 * MIB),
        name="statistics",
    )(grad, stats)


def roots_kernel(flag, stats_ref, roots_ref, out_ref):
    @pl.when(flag[0] == 0)
    def _():
        out_ref[...] = roots_ref[...]

    @pl.when(flag[0] != 0)
    def _():
        row = lax.broadcasted_iota(jnp.int32, (BLOCK, BLOCK), 0)
        col = lax.broadcasted_iota(jnp.int32, (BLOCK, BLOCK), 1)
        identity = (row == col).astype(jnp.float32)

        def times(a, b):
            return mm(a.astype(jnp.bfloat16), b.astype(jnp.bfloat16), ((1,), (0,)))

        def powered(coupled):
            rest = times(coupled, coupled) * 0.0625 - 0.625 * coupled
            rest = times(rest, rest) + 3.125 * rest
            return times(rest, coupled) + 2.44140625 * coupled

        for side in range(2):
            matrix = stats_ref[side]
            scaling = 2.5 / jnp.sqrt(jnp.sum(matrix * matrix, keepdims=True))
            first = matrix * scaling
            second = powered(first)
            third = powered(second)
            both = times(first, second) * 0.0625 - 0.3125 * (first + second) + 1.5625 * identity
            found = 1.25 * both - 0.25 * times(both, third)
            out_ref[side] = found * jnp.sqrt(jnp.sqrt(scaling))


def roots_of(flag, stats, roots):
    whole = pl.BlockSpec(memory_space=pltpu.VMEM)
    return pl.pallas_call(
        roots_kernel,
        out_shape=jax.ShapeDtypeStruct(stats.shape, jnp.float32),
        in_specs=[pl.BlockSpec(memory_space=pltpu.SMEM), whole, whole],
        out_specs=whole,
        compiler_params=pltpu.CompilerParams(vmem_limit_bytes=32 * MIB),
        cost_estimate=cost(16 * 2 * BLOCK**3, 6 * MIB),
        name="roots",
    )(flag, stats, roots)


def place_kernel(count, aliased, number_of, *refs):
    blocks = refs[:count]
    out_ref, sems = refs[count + aliased], refs[count + aliased + 1]
    copies = []
    for i in range(count):
        number = number_of[i]
        row = pl.multiple_of(number // COL_BLK * BLOCK, BLOCK)
        col = pl.multiple_of(number % COL_BLK * BLOCK, BLOCK)
        copy = pltpu.make_async_copy(
            blocks[i], out_ref.at[pl.ds(row, BLOCK), pl.ds(col, BLOCK)], sems.at[i]
        )
        copy.start()
        copies.append(copy)
    for copy in copies:
        copy.wait()


def place(blocks, numbers, into, cols):
    count = len(blocks)
    aliased = into is not None
    anywhere = pl.BlockSpec(memory_space=pl.ANY)
    return pl.pallas_call(
        functools.partial(place_kernel, count, int(aliased)),
        out_shape=jax.ShapeDtypeStruct((FEAT, cols), jnp.bfloat16),
        in_specs=[pl.BlockSpec(memory_space=pltpu.SMEM)] + [anywhere] * (count + aliased),
        out_specs=anywhere,
        scratch_shapes=[pltpu.SemaphoreType.DMA((count,))],
        input_output_aliases={count + 1: 0} if aliased else {},
        cost_estimate=cost(0, count * MIB),
        name="place",
    )(jnp.stack(numbers), *blocks, *([into] if aliased else []))


def body(activations, out_grad, statistics, root_blocks, owner_slots, stagger_phase):
    dp, mp = lax.axis_index("dp"), lax.axis_index("mp")
    y, zh, core = dp // (ZH * CORE), dp // CORE % ZH, dp % CORE
    zl, x = mp // X, mp % X
    step = 1 - 2 * core
    slot_of = owner_slots[0]
    numbers = jnp.arange(BLOCKS, dtype=jnp.int32)
    block_at = jnp.sum(jnp.where(slot_of[:, None] == numbers[None, :], numbers[:, None], 0), axis=0)
    dest_of = jnp.where(slot_of % CORE == core, 0, BLOCKS // 2) + slot_of // CORE
    rows_of = []
    for side in (zl, 1 - zl):
        rows_of += [side * X + (x + shift) % X for shift in (0, -step, step, 2)]
    rows_of = jnp.stack(rows_of)
    groups = jnp.stack([(y + shift) % Y for shift in (0, step, -step, 2)])

    tokens = activations.shape[0]
    by_block = activations.reshape(tokens, ROW_BLK, BLOCK)
    kept, received = [], []
    at = 0
    for rows in CHUNKS:
        own = by_block[:, :, at : at + rows].reshape(tokens, ROW_BLK * rows)
        at += rows
        across = move(own, ZL_SWAP)
        near = move(own, X_NEAR)
        back = move(own, X_BACK)
        far = move(near, X_NEAR)
        across_near = move(across, X_NEAR)
        across_back = move(across, X_BACK)
        across_far = move(far, ZL_SWAP)
        pieces = [own, near, back, far, across, across_near, across_back, across_far]
        keep, send = grad_chunk(pieces, rows_of, dest_of, out_grad, rows)
        mine, to_near, to_back, to_far = chip_sum(keep, move(send, C_SWAP), groups)
        parts = [mine, move(to_near, Y_NEAR), move(to_back, Y_BACK), move(to_far, Y_FAR)]
        keep, send = y_sum(parts, zh[None])
        kept.append(keep)
        received.append(move(send, ZH_SWAP))

    roots = root_blocks[0, 0]
    own, grad = apply_roots(kept, received, roots)

    new_stats = statistics_of(grad, statistics[0, 0])
    flag = ((block_at[dp] + stagger_phase[0]) % 8 == 0).astype(jnp.int32)
    new_roots = roots_of(flag[None], new_stats, roots)

    def slot(shift_y, other_z, other_core):
        where_y = (y + shift_y) % Y
        where_z = 1 - zh if other_z else zh
        where_core = 1 - core if other_core else core
        return (where_y * ZH + where_z) * CORE + where_core

    def both_cores(block, shift_y, other_z):
        return [
            (block, block_at[slot(shift_y, other_z, False)]),
            (move(block, C_SWAP), block_at[slot(-shift_y, other_z, True)]),
        ]

    cols = out_grad.shape[1]
    across = move(own, ZH_SWAP)
    near = move(own, Y_NEAR)
    back = move(own, Y_BACK)
    far = move(near, Y_NEAR)
    across_near = move(across, Y_NEAR)
    across_back = move(across, Y_BACK)
    across_far = move(far, ZH_SWAP)
    update = None
    for stage in (
        [(own, 0, False), (across, 0, True), (near, -step, False), (back, step, False)],
        [(far, 2, False), (across_near, -step, True), (across_back, step, True), (across_far, 2, True)],
    ):
        found = [item for entry in stage for item in both_cores(*entry)]
        update = place([b for b, _ in found], [n for _, n in found], update, cols)
    return (update, new_stats[None, None], new_roots[None, None])


def solution(mesh):
    return jax.shard_map(
        body,
        mesh=mesh,
        in_specs=(
            P(("dp", "mp"), None),
            P("dp", "mp"),
            P("mp", "dp", None, None, None),
            P("mp", "dp", None, None, None),
            P("mp", None),
            P("mp"),
        ),
        out_specs=(P(None, "mp"), P("mp", "dp", None, None, None), P("mp", "dp", None, None, None)),
        check_vma=False,
    )
```

time: 389 us -> 473 us (1.22)
  Pallas kernels: 0 us -> 293 us
  waiting for transfers between devices: 215 us -> 66 us
  starting transfers between devices: 0.3 us -> 76.2 us
  matrix products: 62.9 us -> 0 us
  other arithmetic: 31.8 us -> 0.18 us
  local copies, waits for them, and re-layouts: 54.1 us -> 30.9 us
  between operations: 15.4 us -> 2.43 us
    pallas_call x0 -> x11, Pallas kernels: none -> 293 us  [the longest x2 258 us: place(): pl.pallas_call(functools.partial(place_kernel, count, int(aliased)), out_...]
    all_gather x2 -> x0, waiting for transfers between devices: 115 us -> none  [the longest x1 95.1 us: body(): lax.all_gather(activations, 'mp', axis=0, tiled=True)]
    reduce_scatter x1 -> x0, waiting for transfers between devices: 100 us -> none  [body(): lax.psum_scatter(slotted.astype(jnp.bfloat16), 'dp', scatter_dimension=0,...]
    ppermute x0 -> x39, starting transfers between devices: none -> 76.2 us  [move(): return lax.ppermute(value, ('dp', 'mp'), route)]
    ppermute x0 -> x39, waiting for transfers between devices: none -> 66 us  [move(): return lax.ppermute(value, ('dp', 'mp'), route)]
    dot_general x23 -> x0, matrix products: 62.9 us -> none  [the longest x18 42.5 us: product(): jnp.dot(left_side, right_side, precision=lax.Precision.HIGHEST, preferred...]
    reshape x2 -> x0, local copies, waits for them, and re-layouts: 23 us -> none  [body(): local_grad.reshape(ROW_BLK, BLOCK, column_blocks, BLOCK)]
    select_n x3 -> x0, other arithmetic: 17.6 us -> none  [the longest x2 17.6 us: body(): ordered = jnp.take(all_updates, slot_of, axis=0)]
  transfers between devices with their start and end apart: 3 -> 39, of which waited for: 3 -> 13; matrix products, arithmetic and copies ran while one was open for 13% -> 3% of each run, Pallas kernels for 0% -> 35%
where the time goes in v1:
time: 473 us; the launch traced here: 469 us
  Pallas kernels  293 us (62%)
  starting transfers between devices  76.2 us (16%)
  waiting for transfers between devices  66 us (14%)
  local copies, waits for them, and re-layouts  30.9 us (7%)
    pallas_call x2, Pallas kernels, place(): pl.pallas_call(functools.partial(place_kernel, count, int(aliased)), out_...  258 us
    ppermute x39, starting transfers between devices, move(): return lax.ppermute(value, ('dp', 'mp'), route)  76.2 us
    ppermute x39, waiting for transfers between devices, move(): return lax.ppermute(value, ('dp', 'mp'), route)  66 us
    pallas_call x2, Pallas kernels, grad_chunk(): pl.pallas_call(grad_kernel, out_shape=(half, half), grid_spec=pltpu.Prefe...  19.9 us
    unnamed x57, local copies, waits for them, and re-layouts  18.6 us
    another operation x2, local copies, waits for them, and re-layouts, place(): jnp.stack(numbers)  11.4 us
  transfers between devices with their start and end apart: 39, of which 13 were waited for; matrix products, arithmetic and copies ran while one was open for 3% of the time, Pallas kernels for 35%

profile of v1, /device:TPU:1, one launch (start us, length us, event | category | flops | bytes accessed | tf_op | source)
XLA Modules:
  0.0 469.0 jit_solution(9868884129741436279)
XLA Ops:
  2.5 3.4 collective-permute-start.11
  10.3 3.6 collective-permute-done.11.refs_1_
  14.0 3.4 collective-permute-start.13
  18.2 3.5 collective-permute-start.3
  29.9 3.6 collective-permute-start.17
  34.4 5.7 %collective-permute-done.15.refs_5_ = bf16[128,2048]{1,0:T(8,128)(2,1)} collective-permute-done((bf16[128,2048]{1,0:T(8,128)(2,1)S(1)}, bf16[128,2048]{1,0:T(8,128)(2,1)}, u32[]{:S(2)}, u32[]{:S(2)}) %collective-permute-start.15) | collective-permute-done | bytes 524320 | tf_op jit(solution)/shard_map/ppermute | solution.py:52
  40.0 3.2 collective-permute-start.4
  44.1 6.5 %collective-permute-done.2.refs_3_ = bf16[128,2048]{1,0:T(8,128)(2,1)} collective-permute-done((bf16[128,2048]{1,0:T(8,128)(2,1)S(1)}, bf16[128,2048]{1,0:T(8,128)(2,1)}, u32[]{:S(2)}, u32[]{:S(2)}) %collective-permute-start.2) | collective-permute-done | bytes 524320 | tf_op jit(solution)/shard_map/ppermute | solution.py:52
  60.6 9.8 %grad_chunk.3 = (bf16[8,256,512]{2,1,0:T(8,128)(2,1)S(1)}, bf16[8,256,512]{2,1,0:T(8,128)(2,1)}) custom-call(s32[8]{0:T(128)S(1)} %stack.62.rows_of, s32[16]{0:T(128)S(1)} %fusion.dest_of, bf16[128,2048]{1,0:T(8,128)(2,1)S(1)} %bitcast.34, bf16[128,2048]{1,0:T(8,128)(2,1)S(1)} %copy-done.11, bf16[128,2048]{1,0:T(8,128)(2,1)S(1)} %copy-done.15, ...), custom_call_target="tpu_custom_call" | custom-call | flops 4294967296 | bytes 10485760 | tf_op jit(solution)/shard_map/grad_chunk/pallas_call | solution.py:115
  70.5 6.4 %collective-permute-start.18 = (bf16[8,256,512]{2,1,0:T(8,128)(2,1)}, bf16[8,256,512]{2,1,0:T(8,128)(2,1)}, u32[]{:S(2)}, u32[]{:S(2)}) collective-permute-start(bf16[8,256,512]{2,1,0:T(8,128)(2,1)} %get-tuple-element.29), channel_id=1, source_target_pairs={{0,8},{1,9},{2,10},{3,11},{4,12},{5,13},{6,14},{7,15},{8,0},{9,1},... | collective-permute-start | bytes 6291464 | tf_op jit(solution)/shard_map/ppermute | solution.py:52
  76.9 10.1 %grad_chunk.2 = (bf16[8,256,512]{2,1,0:T(8,128)(2,1)S(1)}, bf16[8,256,512]{2,1,0:T(8,128)(2,1)}) custom-call(s32[8]{0:T(128)S(1)} %stack.62.rows_of, s32[16]{0:T(128)S(1)} %fusion.dest_of, bf16[128,2048]{1,0:T(8,128)(2,1)S(1)} %bitcast.30, bf16[128,2048]{1,0:T(8,128)(2,1)S(1)} %copy-done.9, bf16[128,2048]{1,0:T(8,128)(2,1)} %collective-permute-done.1.refs_2_, ...), custom_call_target="tpu_custom_call" | custom-call | flops 4294967296 | bytes 10485760 | tf_op jit(solution)/shard_map/grad_chunk/pallas_call | solution.py:115
  103.0 4.0 collective-permute-done.19.refs_1_.refs_5_
  107.0 24.0 %collective-permute-done.20.refs_2_.refs_6_ = bf16[2,256,512]{2,1,0:T(8,128)(2,1)S(1)} collective-permute-done((bf16[2,256,512]{2,1,0:T(8,128)(2,1)}, bf16[2,256,512]{2,1,0:T(8,128)(2,1)S(1)}, u32[]{:S(2)}, u32[]{:S(2)}) %collective-permute-start.20) | collective-permute-done | bytes 524320 | tf_op jit(solution)/shard_map/ppermute | solution.py:52
  132.3 3.7 collective-permute-start.23
  142.7 3.8 collective-permute-start.22
  146.5 6.2 %collective-permute-done.22.refs_2_ = bf16[256,512]{1,0:T(8,128)(2,1)S(1)} collective-permute-done((bf16[256,512]{1,0:T(8,128)(2,1)S(1)}, bf16[256,512]{1,0:T(8,128)(2,1)S(1)}, u32[]{:S(2)}, u32[]{:S(2)}) %collective-permute-start.22) | collective-permute-done | bytes 262176 | tf_op jit(solution)/shard_map/ppermute | solution.py:52
  165.7 4.5 collective-permute-done.27.refs_2_
  175.1 4.7 %collective-permute-start.32 = (bf16[512,512]{1,0:T(8,128)(2,1)S(1)}, bf16[512,512]{1,0:T(8,128)(2,1)}, u32[]{:S(2)}, u32[]{:S(2)}) collective-permute-start(bf16[512,512]{1,0:T(8,128)(2,1)S(1)} %collective-permute-done.25.refs_0_), channel_id=1, source_target_pairs={{0,16},{1,17},{2,18},{3,19},{4,20},{5,21},{6,22},{7,23},{8,24},{9,... | collective-permute-start | bytes 1572872 | tf_op jit(solution)/shard_map/ppermute | solution.py:52
  182.1 5.8 %stack.63.number_of = s32[8]{0:T(128)} concatenate(s32[1]{0:T(128)} %get-tuple-element.49, s32[1]{0:T(128)} %get-tuple-element.48, s32[1]{0:T(128)} %get-tuple-element.47, s32[1]{0:T(128)} %get-tuple-element.46, s32[1]{0:T(128)} %get-tuple-element.45, s32[1]{0:T(128)} %get-tuple-element.44, s32[1]{0:T(128)} %get-tuple-element.43, s32[1]{0:T(128)} %get-tuple-element.42), dimensions={0} | concatenate | bytes 64 | tf_op jit(solution)/shard_map/stack | solution.py:316
  187.9 5.6 %stack.48.number_of = s32[8]{0:T(128)} concatenate(s32[1]{0:T(128)} %get-tuple-element.57, s32[1]{0:T(128)} %get-tuple-element.56, s32[1]{0:T(128)} %get-tuple-element.55, s32[1]{0:T(128)} %get-tuple-element.54, s32[1]{0:T(128)} %get-tuple-element.53, s32[1]{0:T(128)} %get-tuple-element.52, s32[1]{0:T(128)} %get-tuple-element.51, s32[1]{0:T(128)} %get-tuple-element.50), dimensions={0} | concatenate | bytes 64 | tf_op jit(solution)/shard_map/stack | solution.py:316
  193.5 8.8 %collective-permute-start.38 = (bf16[512,512]{1,0:T(8,128)(2,1)}, bf16[512,512]{1,0:T(8,128)(2,1)}, u32[]{:S(2)}, u32[]{:S(2)}) collective-permute-start(bf16[512,512]{1,0:T(8,128)(2,1)} %copy-done.24), channel_id=1, source_target_pairs={{0,8},{1,9},{2,10},{3,11},{4,12},{5,13},{6,14},{7,15},{8,0},{9,1},... | collective-permute-start | bytes 1572872 | tf_op jit(solution)/shard_map/ppermute | solution.py:52
  204.5 3.2 statistics.1.stats_ref
  210.9 128.9 %place.2.refs_8_ = bf16[4096,1024]{1,0:T(8,128)(2,1)} custom-call(s32[8]{0:T(128)} %stack.63.number_of, bf16[512,512]{1,0:T(8,128)(2,1)} %copy-done.2, bf16[512,512]{1,0:T(8,128)(2,1)} %copy-done.25, bf16[512,512]{1,0:T(8,128)(2,1)} %collective-permute-done.27.refs_2_, bf16[512,512]{1,0:T(8,128)(2,1)} %collective-permute-done.35.refs_3_, ...), custom_call_target="tpu_custom_call" | custom-call | bytes 8388608 | tf_op jit(solution)/shard_map/place/pallas_call | solution.py:307
  339.9 128.9 %place.3 = bf16[4096,1024]{1,0:T(8,128)(2,1)} custom-call(s32[8]{0:T(128)} %stack.48.number_of, bf16[512,512]{1,0:T(8,128)(2,1)} %copy-done.23, bf16[512,512]{1,0:T(8,128)(2,1)} %collective-permute-done.26.refs_1_, bf16[512,512]{1,0:T(8,128)(2,1)} %collective-permute-done.28.refs_2_, ...), custom_call_target="tpu_custom_call", output_to_operand_aliasing={{}: (9, {})} | custom-call | bytes 8388608 | tf_op jit(solution)/shard_map/place/pallas_call | solution.py:307
  (130 shorter events, 75.3 us)
Async XLA Ops:
  21.7 18.3 %collective-permute-start.15 = (bf16[128,2048]{1,0:T(8,128)(2,1)S(1)}, bf16[128,2048]{1,0:T(8,128)(2,1)}, u32[]{:S(2)}, u32[]{:S(2)}) collective-permute-start(bf16[128,2048]{1,0:T(8,128)(2,1)S(1)} %collective-permute-done.14.refs_4_), channel_id=1, source_target_pairs={{0,1},{1,2},{2,3},{3,0},{4,5},{5,6},{6,7},{7,4},{8,11},{9,8},{10,9... | collective-permute-start | bytes 1572872 | tf_op jit(solution)/shard_map/ppermute | solution.py:52
  23.5 19.8 %collective-permute-start.16 = (bf16[128,2048]{1,0:T(8,128)(2,1)S(1)}, bf16[128,2048]{1,0:T(8,128)(2,1)S(1)}, u32[]{:S(2)}, u32[]{:S(2)}) collective-permute-start(bf16[128,2048]{1,0:T(8,128)(2,1)S(1)} %collective-permute-done.14.refs_4_), channel_id=1, source_target_pairs={{0,3},{1,0},{2,1},{3,2},{4,7},{5,4},{6,5},{7,6},{8,9},{9,10},{10,1... | collective-permute-start | bytes 1572872 | tf_op jit(solution)/shard_map/ppermute | solution.py:52
  24.8 25.8 %collective-permute-start.2 = (bf16[128,2048]{1,0:T(8,128)(2,1)S(1)}, bf16[128,2048]{1,0:T(8,128)(2,1)}, u32[]{:S(2)}, u32[]{:S(2)}) collective-permute-start(bf16[128,2048]{1,0:T(8,128)(2,1)S(1)} %collective-permute-done.refs_1_), channel_id=1, source_target_pairs={{0,1},{1,2},{2,3},{3,0},{4,5},{5,6},{6,7},{7,4},{8,11},{9,8},{10,9... | collective-permute-start | bytes 1572872 | tf_op jit(solution)/shard_map/ppermute | solution.py:52
  29.9 23.1 %collective-permute-start.17 = (bf16[128,2048]{1,0:T(8,128)(2,1)}, bf16[128,2048]{1,0:T(8,128)(2,1)S(1)}, u32[]{:S(2)}, u32[]{:S(2)}) collective-permute-start(bf16[128,2048]{1,0:T(8,128)(2,1)} %collective-permute-done.13.refs_3_), channel_id=1, source_target_pairs={{0,4},{1,5},{2,6},{3,7},{4,0},{5,1},{6,2},{7,3},{8,12},{9,13},{10,... | collective-permute-start | bytes 1572872 | tf_op jit(solution)/shard_map/ppermute | solution.py:52
  33.5 43.3 %collective-permute-start.1 = (bf16[128,2048]{1,0:T(8,128)(2,1)S(1)}, bf16[128,2048]{1,0:T(8,128)(2,1)}, u32[]{:S(2)}, u32[]{:S(2)}) collective-permute-start(bf16[128,2048]{1,0:T(8,128)(2,1)S(1)} %bitcast.29), channel_id=1, source_target_pairs={{0,3},{1,0},{2,1},{3,2},{4,7},{5,4},{6,5},{7,6},{8,9},{9,10},{10,1... | collective-permute-start | bytes 1572872 | tf_op jit(solution)/shard_map/ppermute | solution.py:52
  40.0 36.8 %collective-permute-start.4 = (bf16[128,2048]{1,0:T(8,128)(2,1)}, bf16[128,2048]{1,0:T(8,128)(2,1)}, u32[]{:S(2)}, u32[]{:S(2)}) collective-permute-start(bf16[128,2048]{1,0:T(8,128)(2,1)} %collective-permute-done.3.refs_4_), channel_id=1, source_target_pairs={{0,1},{1,2},{2,3},{3,0},{4,5},{5,6},{6,7},{7,4},{8,11},{9,8},{10,9... | collective-permute-start | bytes 1572872 | tf_op jit(solution)/shard_map/ppermute | solution.py:52
  44.1 32.8 %collective-permute-start.5 = (bf16[128,2048]{1,0:T(8,128)(2,1)}, bf16[128,2048]{1,0:T(8,128)(2,1)}, u32[]{:S(2)}, u32[]{:S(2)}) collective-permute-start(bf16[128,2048]{1,0:T(8,128)(2,1)} %collective-permute-done.3.refs_4_), channel_id=1, source_target_pairs={{0,3},{1,0},{2,1},{3,2},{4,7},{5,4},{6,5},{7,6},{8,9},{9,10},{10,1... | collective-permute-start | bytes 1572872 | tf_op jit(solution)/shard_map/ppermute | solution.py:52
  50.6 26.3 %collective-permute-start.6 = (bf16[128,2048]{1,0:T(8,128)(2,1)}, bf16[128,2048]{1,0:T(8,128)(2,1)}, u32[]{:S(2)}, u32[]{:S(2)}) collective-permute-start(bf16[128,2048]{1,0:T(8,128)(2,1)} %collective-permute-done.2.refs_3_), channel_id=1, source_target_pairs={{0,4},{1,5},{2,6},{3,7},{4,0},{5,1},{6,2},{7,3},{8,12},{9,13},{10,... | collective-permute-start | bytes 1572872 | tf_op jit(solution)/shard_map/ppermute | solution.py:52
  70.5 17.9 %collective-permute-start.18 = (bf16[8,256,512]{2,1,0:T(8,128)(2,1)}, bf16[8,256,512]{2,1,0:T(8,128)(2,1)}, u32[]{:S(2)}, u32[]{:S(2)}) collective-permute-start(bf16[8,256,512]{2,1,0:T(8,128)(2,1)} %get-tuple-element.29), channel_id=1, source_target_pairs={{0,8},{1,9},{2,10},{3,11},{4,12},{5,13},{6,14},{7,15},{8,0},{9,1},... | collective-permute-start | bytes 6291464 | tf_op jit(solution)/shard_map/ppermute | solution.py:52
  94.2 36.8 %collective-permute-start.20 = (bf16[2,256,512]{2,1,0:T(8,128)(2,1)}, bf16[2,256,512]{2,1,0:T(8,128)(2,1)S(1)}, u32[]{:S(2)}, u32[]{:S(2)}) collective-permute-start(bf16[2,256,512]{2,1,0:T(8,128)(2,1)} %get-tuple-element.32), channel_id=1, source_target_pairs={{0,96},{1,97},{2,98},{3,99},{4,100},{5,101},{6,102},{7,103},{8,40}... | collective-permute-start | bytes 1572872 | tf_op jit(solution)/shard_map/ppermute | solution.py:52
  94.2 36.8 %collective-permute-start.21 = (bf16[2,256,512]{2,1,0:T(8,128)(2,1)}, bf16[2,256,512]{2,1,0:T(8,128)(2,1)}, u32[]{:S(2)}, u32[]{:S(2)}) collective-permute-start(bf16[2,256,512]{2,1,0:T(8,128)(2,1)} %get-tuple-element.33), channel_id=1, source_target_pairs={{0,64},{1,65},{2,66},{3,67},{4,68},{5,69},{6,70},{7,71},{8,72},{9,... | collective-permute-start | bytes 1572872 | tf_op jit(solution)/shard_map/ppermute | solution.py:52
  99.0 37.0 %collective-permute-start.10 = (bf16[2,256,512]{2,1,0:T(8,128)(2,1)}, bf16[2,256,512]{2,1,0:T(8,128)(2,1)S(1)}, u32[]{:S(2)}, u32[]{:S(2)}) collective-permute-start(bf16[2,256,512]{2,1,0:T(8,128)(2,1)} %get-tuple-element.26), channel_id=1, source_target_pairs={{0,64},{1,65},{2,66},{3,67},{4,68},{5,69},{6,70},{7,71},{8,72},{9,... | collective-permute-start | bytes 1572872 | tf_op jit(solution)/shard_map/ppermute | solution.py:52
  100.3 38.1 %collective-permute-start.8 = (bf16[2,256,512]{2,1,0:T(8,128)(2,1)}, bf16[2,256,512]{2,1,0:T(8,128)(2,1)S(1)}, u32[]{:S(2)}, u32[]{:S(2)}) collective-permute-start(bf16[2,256,512]{2,1,0:T(8,128)(2,1)} %get-tuple-element.24), channel_id=1, source_target_pairs={{0,32},{1,33},{2,34},{3,35},{4,36},{5,37},{6,38},{7,39},{8,104},{9... | collective-permute-start | bytes 1572872 | tf_op jit(solution)/shard_map/ppermute | solution.py:52
  107.0 34.3 %collective-permute-start.9 = (bf16[2,256,512]{2,1,0:T(8,128)(2,1)}, bf16[2,256,512]{2,1,0:T(8,128)(2,1)}, u32[]{:S(2)}, u32[]{:S(2)}) collective-permute-start(bf16[2,256,512]{2,1,0:T(8,128)(2,1)} %get-tuple-element.25), channel_id=1, source_target_pairs={{0,96},{1,97},{2,98},{3,99},{4,100},{5,101},{6,102},{7,103},{8,40}... | collective-permute-start | bytes 1572872 | tf_op jit(solution)/shard_map/ppermute | solution.py:52
  170.1 23.3 %collective-permute-start.35 = (bf16[512,512]{1,0:T(8,128)(2,1)}, bf16[512,512]{1,0:T(8,128)(2,1)}, u32[]{:S(2)}, u32[]{:S(2)}) collective-permute-start(bf16[512,512]{1,0:T(8,128)(2,1)} %collective-permute-done.27.refs_2_), channel_id=1, source_target_pairs={{0,8},{1,9},{2,10},{3,11},{4,12},{5,13},{6,14},{7,15},{8,0},{9,1},... | collective-permute-start | bytes 1572872 | tf_op jit(solution)/shard_map/ppermute | solution.py:52
  172.0 30.3 %collective-permute-start.36 = (bf16[512,512]{1,0:T(8,128)(2,1)}, bf16[512,512]{1,0:T(8,128)(2,1)}, u32[]{:S(2)}, u32[]{:S(2)}) collective-permute-start(bf16[512,512]{1,0:T(8,128)(2,1)} %collective-permute-done.24.refs_4_), channel_id=1, source_target_pairs={{0,8},{1,9},{2,10},{3,11},{4,12},{5,13},{6,14},{7,15},{8,0},{9,1},... | collective-permute-start | bytes 1572872 | tf_op jit(solution)/shard_map/ppermute | solution.py:52
  172.0 30.3 %collective-permute-start.28 = (bf16[512,512]{1,0:T(8,128)(2,1)}, bf16[512,512]{1,0:T(8,128)(2,1)}, u32[]{:S(2)}, u32[]{:S(2)}) collective-permute-start(bf16[512,512]{1,0:T(8,128)(2,1)} %collective-permute-done.27.refs_2_), channel_id=1, source_target_pairs={{0,32},{1,33},{2,34},{3,35},{4,36},{5,37},{6,38},{7,39},{8,104},{9... | collective-permute-start | bytes 1572872 | tf_op jit(solution)/shard_map/ppermute | solution.py:52
  173.2 29.5 %collective-permute-start.30 = (bf16[512,512]{1,0:T(8,128)(2,1)}, bf16[512,512]{1,0:T(8,128)(2,1)}, u32[]{:S(2)}, u32[]{:S(2)}) collective-permute-start(bf16[512,512]{1,0:T(8,128)(2,1)} %collective-permute-done.27.refs_2_), channel_id=1, source_target_pairs={{0,96},{1,97},{2,98},{3,99},{4,100},{5,101},{6,102},{7,103},{8,40}... | collective-permute-start | bytes 1572872 | tf_op jit(solution)/shard_map/ppermute | solution.py:52
  175.1 27.7 %collective-permute-start.32 = (bf16[512,512]{1,0:T(8,128)(2,1)S(1)}, bf16[512,512]{1,0:T(8,128)(2,1)}, u32[]{:S(2)}, u32[]{:S(2)}) collective-permute-start(bf16[512,512]{1,0:T(8,128)(2,1)S(1)} %collective-permute-done.25.refs_0_), channel_id=1, source_target_pairs={{0,16},{1,17},{2,18},{3,19},{4,20},{5,21},{6,22},{7,23},{8,24},{9,... | collective-permute-start | bytes 1572872 | tf_op jit(solution)/shard_map/ppermute | solution.py:52
  193.5 17.5 %collective-permute-start.38 = (bf16[512,512]{1,0:T(8,128)(2,1)}, bf16[512,512]{1,0:T(8,128)(2,1)}, u32[]{:S(2)}, u32[]{:S(2)}) collective-permute-start(bf16[512,512]{1,0:T(8,128)(2,1)} %copy-done.24), channel_id=1, source_target_pairs={{0,8},{1,9},{2,10},{3,11},{4,12},{5,13},{6,14},{7,15},{8,0},{9,1},... | collective-permute-start | bytes 1572872 | tf_op jit(solution)/shard_map/ppermute | solution.py:52
  202.2 137.6 %collective-permute-start.26 = (bf16[512,512]{1,0:T(8,128)(2,1)S(1)}, bf16[512,512]{1,0:T(8,128)(2,1)}, u32[]{:S(2)}, u32[]{:S(2)}) collective-permute-start(bf16[512,512]{1,0:T(8,128)(2,1)S(1)} %collective-permute-done.25.refs_0_), channel_id=1, source_target_pairs={{0,8},{1,9},{2,10},{3,11},{4,12},{5,13},{6,14},{7,15},{8,0},{9,1},... | collective-permute-start | bytes 1572872 | tf_op jit(solution)/shard_map/ppermute | solution.py:52
  202.3 137.5 %collective-permute-start.29 = (bf16[512,512]{1,0:T(8,128)(2,1)}, bf16[512,512]{1,0:T(8,128)(2,1)}, u32[]{:S(2)}, u32[]{:S(2)}) collective-permute-start(bf16[512,512]{1,0:T(8,128)(2,1)} %collective-permute-done.28.refs_2_), channel_id=1, source_target_pairs={{0,8},{1,9},{2,10},{3,11},{4,12},{5,13},{6,14},{7,15},{8,0},{9,1},... | collective-permute-start | bytes 1572872 | tf_op jit(solution)/shard_map/ppermute | solution.py:52
  202.8 137.1 %collective-permute-start.31 = (bf16[512,512]{1,0:T(8,128)(2,1)}, bf16[512,512]{1,0:T(8,128)(2,1)}, u32[]{:S(2)}, u32[]{:S(2)}) collective-permute-start(bf16[512,512]{1,0:T(8,128)(2,1)} %collective-permute-done.30.refs_4_), channel_id=1, source_target_pairs={{0,8},{1,9},{2,10},{3,11},{4,12},{5,13},{6,14},{7,15},{8,0},{9,1},... | collective-permute-start | bytes 1572872 | tf_op jit(solution)/shard_map/ppermute | solution.py:52
  202.8 137.0 %collective-permute-start.33 = (bf16[512,512]{1,0:T(8,128)(2,1)}, bf16[512,512]{1,0:T(8,128)(2,1)}, u32[]{:S(2)}, u32[]{:S(2)}) collective-permute-start(bf16[512,512]{1,0:T(8,128)(2,1)} %collective-permute-done.32.refs_6_), channel_id=1, source_target_pairs={{0,8},{1,9},{2,10},{3,11},{4,12},{5,13},{6,14},{7,15},{8,0},{9,1},... | collective-permute-start | bytes 1572872 | tf_op jit(solution)/shard_map/ppermute | solution.py:52
  (42 other events, 440.7 us)

commit v2 on v1

v2 whole, which is shorter than its diff:
```python
import functools

import jax
import jax.numpy as jnp
from jax import lax
from jax.experimental import pallas as pl
from jax.experimental.pallas import tpu as pltpu
from jax.sharding import PartitionSpec as P

FEAT = 4096
BLOCK = 512
ROW_BLK = 8
COL_BLK = 2
BLOCKS = ROW_BLK * COL_BLK
CHUNKS = (256, 256)
Y, ZH, CORE, ZL, X = 4, 2, 2, 2, 4
N_MP = ZL * X
MIB = 1 << 20


def device_of(y, zh, core, zl, x):
    return ((y * ZH + zh) * CORE + core) * N_MP + zl * X + x


def pairs(move):
    out = []
    for y in range(Y):
        for zh in range(ZH):
            for core in range(CORE):
                for zl in range(ZL):
                    for x in range(X):
                        here = (y, zh, core, zl, x)
                        out.append((device_of(*here), device_of(*move(*here))))
    return out


def way(core):
    return 1 if core == 0 else -1


X_NEAR = pairs(lambda y, zh, c, zl, x: (y, zh, c, zl, (x + way(c)) % X))
X_BACK = pairs(lambda y, zh, c, zl, x: (y, zh, c, zl, (x - way(c)) % X))
X_FAR = pairs(lambda y, zh, c, zl, x: (y, zh, c, zl, (x + 2) % X))
Y_NEAR = pairs(lambda y, zh, c, zl, x: ((y + way(c)) % Y, zh, c, zl, x))
Y_BACK = pairs(lambda y, zh, c, zl, x: ((y - way(c)) % Y, zh, c, zl, x))
Y_FAR = pairs(lambda y, zh, c, zl, x: ((y + 2) % Y, zh, c, zl, x))
Y_NEAR_Z = pairs(lambda y, zh, c, zl, x: ((y + way(c)) % Y, 1 - zh, c, zl, x))
Y_BACK_Z = pairs(lambda y, zh, c, zl, x: ((y - way(c)) % Y, 1 - zh, c, zl, x))
Y_FAR_Z = pairs(lambda y, zh, c, zl, x: ((y + 2) % Y, 1 - zh, c, zl, x))
ZL_SWAP = pairs(lambda y, zh, c, zl, x: (y, zh, c, 1 - zl, x))
ZH_SWAP = pairs(lambda y, zh, c, zl, x: (y, 1 - zh, c, zl, x))
C_SWAP = pairs(lambda y, zh, c, zl, x: (y, zh, 1 - c, zl, x))


def move(value, route):
    return lax.ppermute(value, ("dp", "mp"), route)


def cost(flops, moved):
    return pl.CostEstimate(flops=10**12, bytes_accessed=10**12, transcendentals=0)


PARAMS = pltpu.CompilerParams(vmem_limit_bytes=16 * MIB)
ANYWHERE = pl.BlockSpec(memory_space=pl.ANY)
SCALARS = pl.BlockSpec(memory_space=pltpu.SMEM)
WHOLE = pl.BlockSpec(memory_space=pltpu.VMEM)


def mm(a, b, contract):
    return lax.dot_general(a, b, (contract, ((), ())), preferred_element_type=jnp.float32)


def place_here():
    dp, mp = lax.axis_index("dp"), lax.axis_index("mp")
    return dp >> 2, (dp >> 1) & 1, dp & 1, mp >> 2, mp & 3


def hops(core):
    step = 1 - 2 * core
    return 0, -step, step, 2


def block_in(slots, slot):
    number = 0
    for i in range(BLOCKS):
        number = jnp.where(slots[i] == slot, i, number)
    return number


def split(value):
    high = value.astype(jnp.bfloat16)
    return high, (value - high.astype(jnp.float32)).astype(jnp.bfloat16)


def mm3(a, b, contract=((1,), (0,))):
    a_high, a_low = a
    b_high, b_low = b
    return (
        mm(a_high, b_high, contract) + mm(a_high, b_low, contract) + mm(a_low, b_high, contract)
    )


def grad_kernel(rows, span, slots, *refs):
    pieces = refs[:N_MP]
    _, _, core, zl, x = place_here()
    rows_of = [side * X + ((x + hop) & 3) for side in (zl, 1 - zl) for hop in hops(core)]
    og_ref, keep_ref, send_ref, gathered, og, tiles, og_sems, in_sems, sems = refs[N_MP:]
    part = pieces[0].shape[1]
    steps = ROW_BLK // span
    size = span * rows

    def og_copy(col):
        cols = pl.ds(col * BLOCK, BLOCK)
        return pltpu.make_async_copy(og_ref.at[:, cols], og.at[:, cols], og_sems.at[col])

    def piece_copies(step):
        lines = pl.ds(step * size, size)
        return [
            pltpu.make_async_copy(
                pieces[i].at[lines],
                gathered.at[lines, pl.ds(pl.multiple_of(rows_of[i] * part, part), part)],
                in_sems.at[step, i],
            )
            for i in range(N_MP)
        ]

    arrivals = [piece_copies(step) for step in range(steps)]
    for step in range(steps):
        if step < COL_BLK:
            og_copy(step).start()
        for copy in arrivals[step]:
            copy.start()
    for step in range(steps):
        for copy in arrivals[step]:
            copy.wait()
        for col in range(COL_BLK):
            if step == 0:
                og_copy(col).wait()
            grad = mm(
                gathered[step * size : (step + 1) * size],
                og[:, col * BLOCK : (col + 1) * BLOCK],
                ((1,), (0,)),
            ).astype(jnp.bfloat16)
            for row in range(span):
                number = (step * span + row) * COL_BLK + col
                slot = slots[number]
                dest = jnp.where((slot & 1) == core, 0, BLOCKS // 2) + (slot >> 1)
                tiles[number] = grad[row * rows : (row + 1) * rows]

                @pl.when(dest < BLOCKS // 2)
                def _():
                    pltpu.make_async_copy(
                        tiles.at[number], keep_ref.at[dest], sems.at[number]
                    ).start()

                @pl.when(dest >= BLOCKS // 2)
                def _():
                    pltpu.make_async_copy(
                        tiles.at[number], send_ref.at[dest - BLOCKS // 2], sems.at[number]
                    ).start()

    for number in range(BLOCKS):
        pltpu.make_async_copy(tiles.at[number], keep_ref.at[0], sems.at[number]).wait()


def grad_chunk(pieces, slot_of, og, rows):
    tokens, cols = og.shape
    span = 2 if rows > 128 else 4
    steps = ROW_BLK // span
    half = jax.ShapeDtypeStruct((BLOCKS // 2, rows, BLOCK), jnp.bfloat16)
    return pl.pallas_call(
        functools.partial(grad_kernel, rows, span),
        out_shape=(half, half),
        in_specs=[SCALARS] + [ANYWHERE] * (N_MP + 1),
        out_specs=(ANYWHERE, ANYWHERE),
        scratch_shapes=[
            pltpu.VMEM((ROW_BLK * rows, tokens), jnp.bfloat16),
            pltpu.VMEM((tokens, cols), jnp.bfloat16),
            pltpu.VMEM((BLOCKS, rows, BLOCK), jnp.bfloat16),
            pltpu.SemaphoreType.DMA((COL_BLK,)),
            pltpu.SemaphoreType.DMA((steps, N_MP)),
            pltpu.SemaphoreType.DMA((BLOCKS,)),
        ],
        compiler_params=PARAMS,
        cost_estimate=cost(2 * tokens * cols * rows * ROW_BLK, 2 * 5 * MIB),
        name="grad_chunk",
    )(slot_of, *pieces, og)


def chip_kernel(count, by_y, keep_ref, recv_ref, *refs):
    y, zh, core, _, _ = place_here()
    along = [((y - hop) & 3) * ZH for hop in hops(core)]
    if by_y:
        order = [at + j for at in along for j in range(ZH)]
    else:
        order = [at + j for j in (zh, 1 - zh) for at in along]
    outs = refs[:count]
    keep, recv, total, keep_sems, recv_sems, out_sems = refs[count:]
    places = Y * ZH
    each = places // count
    arrivals, copies = [], []
    for i in range(places):
        pair = [
            pltpu.make_async_copy(keep_ref.at[order[i]], keep.at[i], keep_sems.at[i]),
            pltpu.make_async_copy(recv_ref.at[order[i]], recv.at[i], recv_sems.at[i]),
        ]
        for copy in pair:
            copy.start()
        arrivals.append(pair)
    for i in range(places):
        for copy in arrivals[i]:
            copy.wait()
        total[i] = (keep[i].astype(jnp.float32) + recv[i].astype(jnp.float32)).astype(jnp.bfloat16)
        copy = pltpu.make_async_copy(total.at[i], outs[i // each].at[i % each], out_sems.at[i])
        copy.start()
        copies.append(copy)
    for copy in copies:
        copy.wait()


def chip_sum(keep, received, by_y):
    count = Y if by_y else Y * ZH
    rows = keep.shape[1]
    out = jax.ShapeDtypeStruct((Y * ZH // count, rows, BLOCK), jnp.bfloat16)
    held = pltpu.VMEM((Y * ZH, rows, BLOCK), jnp.bfloat16)
    return pl.pallas_call(
        functools.partial(chip_kernel, count, by_y),
        out_shape=(out,) * count,
        in_specs=[ANYWHERE, ANYWHERE],
        out_specs=(ANYWHERE,) * count,
        scratch_shapes=[held] * 3 + [pltpu.SemaphoreType.DMA((Y * ZH,))] * 3,
        compiler_params=PARAMS,
        cost_estimate=cost(MIB, keep.size * 6),
        name="chip_sum",
    )(keep, received)


def y_kernel(*refs):
    _, zh, _, _, _ = place_here()
    parts = refs[:Y]
    keep_ref, send_ref, held, keep, send, in_sems, out_sems = refs[Y:]
    arrivals = []
    for j in range(ZH):
        at = zh if j else 1 - zh
        arrivals.append(
            [pltpu.make_async_copy(parts[i].at[at], held.at[j, i], in_sems.at[j, i]) for i in range(Y)]
        )
        for copy in arrivals[j]:
            copy.start()
    out = [
        pltpu.make_async_copy(send, send_ref, out_sems.at[0]),
        pltpu.make_async_copy(keep, keep_ref, out_sems.at[1]),
    ]
    for j in range(ZH):
        for copy in arrivals[j]:
            copy.wait()
        total = sum(held[j, i].astype(jnp.float32) for i in range(Y))
        if j:
            keep[...] = total
        else:
            send[...] = total.astype(jnp.bfloat16)
        out[j].start()
    for copy in out:
        copy.wait()


def y_sum(parts):
    rows = parts[0].shape[1]
    return pl.pallas_call(
        y_kernel,
        out_shape=(
            jax.ShapeDtypeStruct((rows, BLOCK), jnp.float32),
            jax.ShapeDtypeStruct((rows, BLOCK), jnp.bfloat16),
        ),
        in_specs=[ANYWHERE] * Y,
        out_specs=(ANYWHERE, ANYWHERE),
        scratch_shapes=[
            pltpu.VMEM((ZH, Y, rows, BLOCK), jnp.bfloat16),
            pltpu.VMEM((rows, BLOCK), jnp.float32),
            pltpu.VMEM((rows, BLOCK), jnp.bfloat16),
            pltpu.SemaphoreType.DMA((ZH, Y)),
            pltpu.SemaphoreType.DMA((ZH,)),
        ],
        compiler_params=PARAMS,
        cost_estimate=cost(MIB, rows * BLOCK * 22),
        name="y_sum",
    )(*parts)


def apply_kernel(counts, *refs):
    terms = refs[: sum(counts)]
    roots_ref, update_ref, grad_ref = refs[sum(counts) :]
    at = first = 0
    for rows, count in zip(CHUNKS, counts, strict=True):
        grad_ref[at : at + rows] = sum(
            term[...].astype(jnp.float32) for term in terms[first : first + count]
        )
        at += rows
        first += count
    grad = split(grad_ref[...])
    right = mm3(grad, split(roots_ref[1]))
    update_ref[...] = mm3(split(roots_ref[0]), split(right)).astype(jnp.bfloat16)


def apply_roots(terms, roots):
    counts = [len(group) for group in terms]
    return pl.pallas_call(
        functools.partial(apply_kernel, counts),
        out_shape=(
            jax.ShapeDtypeStruct((BLOCK, BLOCK), jnp.bfloat16),
            jax.ShapeDtypeStruct((BLOCK, BLOCK), jnp.float32),
        ),
        in_specs=[WHOLE] * (sum(counts) + 1),
        out_specs=(WHOLE, WHOLE),
        compiler_params=pltpu.CompilerParams(vmem_limit_bytes=16 * MIB),
        cost_estimate=cost(6 * 2 * BLOCK**3, 5 * MIB),
        name="apply_roots",
    )(*[term for group in terms for term in group], roots)


def stats_kernel(grad_ref, stats_ref, out_ref):
    grad = split(grad_ref[...])
    out_ref[0] = 0.95 * stats_ref[0] + mm3(grad, grad, ((1,), (1,)))
    out_ref[1] = 0.95 * stats_ref[1] + mm3(grad, grad, ((0,), (0,)))


def statistics_of(grad, stats):
    return pl.pallas_call(
        stats_kernel,
        out_shape=jax.ShapeDtypeStruct(stats.shape, jnp.float32),
        in_specs=[WHOLE] * 2,
        out_specs=WHOLE,
        compiler_params=PARAMS,
        cost_estimate=cost(6 * 2 * BLOCK**3, 5 * MIB),
        name="statistics",
    )(grad, stats)


def roots_kernel(slots, phase, stats_ref, roots_ref, out_ref):
    y, zh, core, _, _ = place_here()
    number = block_in(slots, (y * ZH + zh) * CORE + core)
    refreshed = ((number + phase[0]) & 7) == 0

    @pl.when(jnp.logical_not(refreshed))
    def _():
        out_ref[...] = roots_ref[...]

    @pl.when(refreshed)
    def _():
        row = lax.broadcasted_iota(jnp.int32, (BLOCK, BLOCK), 0)
        col = lax.broadcasted_iota(jnp.int32, (BLOCK, BLOCK), 1)
        identity = (row == col).astype(jnp.float32)

        def times(a, b):
            return mm(a.astype(jnp.bfloat16), b.astype(jnp.bfloat16), ((1,), (0,)))

        def powered(coupled):
            rest = times(coupled, coupled) * 0.0625 - 0.625 * coupled
            rest = times(rest, rest) + 3.125 * rest
            return times(rest, coupled) + 2.44140625 * coupled

        for side in range(2):
            matrix = stats_ref[side]
            scaling = 2.5 / jnp.sqrt(jnp.sum(matrix * matrix, keepdims=True))
            first = matrix * scaling
            second = powered(first)
            third = powered(second)
            both = times(first, second) * 0.0625 - 0.3125 * (first + second) + 1.5625 * identity
            found = 1.25 * both - 0.25 * times(both, third)
            out_ref[side] = found * jnp.sqrt(jnp.sqrt(scaling))


def roots_of(slot_of, phase, stats, roots):
    return pl.pallas_call(
        roots_kernel,
        out_shape=jax.ShapeDtypeStruct(stats.shape, jnp.float32),
        in_specs=[SCALARS, SCALARS, WHOLE, WHOLE],
        out_specs=WHOLE,
        compiler_params=PARAMS,
        cost_estimate=cost(16 * 2 * BLOCK**3, 6 * MIB),
        name="roots",
    )(slot_of, phase, stats, roots)


def place_kernel(whence, aliased, slots, *refs):
    y, zh, core, _, _ = place_here()
    count = len(whence)
    blocks = refs[:count]
    out_ref, held, in_sems, out_sems = refs[count + aliased :]
    arrivals = [
        pltpu.make_async_copy(blocks[i], held.at[i], in_sems.at[i]) for i in range(count)
    ]
    for copy in arrivals:
        copy.start()
    copies = []
    for i in range(count):
        hop, other_z, other_core = whence[i]
        there = 1 - core if other_core else core
        at_z = 1 - zh if other_z else zh
        number = block_in(slots, (((y + hops(there)[hop]) & 3) * ZH + at_z) * CORE + there)
        row = pl.multiple_of(number // COL_BLK * BLOCK, BLOCK)
        col = pl.multiple_of(number % COL_BLK * BLOCK, BLOCK)
        arrivals[i].wait()
        copy = pltpu.make_async_copy(
            held.at[i], out_ref.at[pl.ds(row, BLOCK), pl.ds(col, BLOCK)], out_sems.at[i]
        )
        copy.start()
        copies.append(copy)
    for copy in copies:
        copy.wait()


def place(found, slot_of, into, cols):
    blocks, whence = [entry[0] for entry in found], [entry[1:] for entry in found]
    count = len(found)
    aliased = into is not None
    return pl.pallas_call(
        functools.partial(place_kernel, whence, int(aliased)),
        out_shape=jax.ShapeDtypeStruct((FEAT, cols), jnp.bfloat16),
        in_specs=[SCALARS] + [ANYWHERE] * (count + aliased),
        out_specs=ANYWHERE,
        scratch_shapes=[
            pltpu.VMEM((count, BLOCK, BLOCK), jnp.bfloat16),
            pltpu.SemaphoreType.DMA((count,)),
            pltpu.SemaphoreType.DMA((count,)),
        ],
        input_output_aliases={count + 1: 0} if aliased else {},
        compiler_params=PARAMS,
        cost_estimate=cost(0, count * MIB),
        name="place",
    )(slot_of, *blocks, *([into] if aliased else []))


def after(value, *others):
    return lax.optimization_barrier((value, *others))[0]


def body(activations, out_grad, statistics, root_blocks, owner_slots, stagger_phase):
    slot_of = owner_slots[0]
    roots = root_blocks[0, 0]
    tokens = activations.shape[0]
    cols = out_grad.shape[1]
    by_block = activations.reshape(tokens, ROW_BLK, BLOCK)
    owns = []
    at = 0
    for rows in CHUNKS:
        owns.append(by_block[:, :, at : at + rows].transpose(1, 2, 0).reshape(ROW_BLK * rows, tokens))
        at += rows

    far_a, across_a = move(owns[0], X_FAR), move(owns[0], ZL_SWAP)
    near_a, back_a = move(owns[0], X_NEAR), move(owns[0], X_BACK)
    across_b = move(after(owns[1], across_a), ZL_SWAP)
    rest_a = [move(across_a, X_NEAR), move(across_a, X_BACK), move(far_a, ZL_SWAP)]
    rest_a[2] = after(rest_a[2], across_b)
    own_b = after(owns[1], far_a)
    far_b, near_b, back_b = move(own_b, X_FAR), move(own_b, X_NEAR), move(own_b, X_BACK)

    pieces = [owns[0], near_a, back_a, far_a, across_a, *rest_a]
    keep_a, send_a = grad_chunk(pieces, slot_of, out_grad, CHUNKS[0])
    swapped_a = move(after(send_a, near_b, back_b), C_SWAP)
    across_b = after(across_b, keep_a)
    rest_b = [move(across_b, X_NEAR), move(across_b, X_BACK), move(far_b, ZL_SWAP)]
    mine, *to = chip_sum(keep_a, swapped_a, True)
    parts = [mine, move(to[0], Y_NEAR), move(to[1], Y_BACK), move(to[2], Y_FAR)]

    pieces = [owns[1], near_b, back_b, far_b, across_b, *rest_b]
    keep_b, send_b = grad_chunk(pieces, slot_of, out_grad, CHUNKS[1])
    swapped_b = move(after(send_b, *parts[1:]), C_SWAP)
    keep_a, send_a = y_sum(parts)
    mine, *to = chip_sum(keep_b, after(swapped_b, send_a), False)
    to = [part[0] for part in to]
    near, back, far = move(to[0], Y_NEAR), move(to[1], Y_BACK), move(to[2], Y_FAR)
    terms_b = [mine[0], near, back, far, move(to[3], ZH_SWAP), move(to[6], Y_FAR_Z)]
    terms_b += [move(after(to[4], near), Y_NEAR_Z), move(after(to[5], back), Y_BACK_Z)]
    terms_a = [keep_a, move(send_a, ZH_SWAP)]

    own, grad = apply_roots([terms_a, terms_b], roots)

    across, near, back = move(own, ZH_SWAP), move(own, Y_NEAR), move(own, Y_BACK)
    own_other = move(own, C_SWAP)
    new_stats = statistics_of(grad, statistics[0, 0])
    near = after(near, new_stats, own_other)
    far = move(near, Y_NEAR)
    across, far_ = after(across, far), after(far, back)
    across_near, across_back = move(across, Y_NEAR), move(across, Y_BACK)
    across_far = move(far_, ZH_SWAP)
    new_roots = roots_of(slot_of, stagger_phase, after(new_stats, far), roots)
    found = [(own, 0, False, False), (own_other, 0, False, True)]
    found += [(near, 1, False, False), (move(near, C_SWAP), 1, False, True)]
    found += [(back, 2, False, False), (move(back, C_SWAP), 2, False, True)]
    found += [(across, 0, True, False), (far, 3, False, False)]
    update = place(found, slot_of, None, cols)

    found = []
    for block, hop in ((across_near, 1), (across_back, 2), (across_far, 3)):
        block = after(block, update, new_roots)
        found += [(block, hop, True, False), (move(block, C_SWAP), hop, True, True)]
    found.append((move(after(across, update, new_roots), C_SWAP), 0, True, True))
    found.append((move(after(far, update, new_roots), C_SWAP), 3, False, True))
    update = place(found, slot_of, update, cols)
    return (update, new_stats[None, None], new_roots[None, None])


def solution(mesh):
    return jax.shard_map(
        body,
        mesh=mesh,
        in_specs=(
            P(("dp", "mp"), None),
            P("dp", "mp"),
            P("mp", "dp", None, None, None),
            P("mp", "dp", None, None, None),
            P("mp", None),
            P("mp"),
        ),
        out_specs=(P(None, "mp"), P("mp", "dp", None, None, None), P("mp", "dp", None, None, None)),
        check_vma=False,
    )
```

time: 473 us -> 203 us (0.43)
  Pallas kernels: 293 us -> 38.6 us
  waiting for transfers between devices: 66 us -> 100 us
  local copies, waits for them, and re-layouts: 30.9 us -> 4.23 us
  starting transfers between devices: 76.2 us -> 58.2 us
    pallas_call x7, Pallas kernels: 286 us -> 31.8 us  [the longest x2 17.2 us: grad_chunk(): pl.pallas_call(functools.partial(grad_kernel, rows, span), out_shape=(hal...]
    ppermute x39 -> x42, waiting for transfers between devices: 66 us -> 100 us  [move(): return lax.ppermute(value, ('dp', 'mp'), route)]
    ppermute x39 -> x42, starting transfers between devices: 76.2 us -> 58.2 us  [move(): return lax.ppermute(value, ('dp', 'mp'), route)]
    unnamed x57 -> x10, local copies, waits for them, and re-layouts: 18.6 us -> 1.61 us
    another operation x3 -> x0, local copies, waits for them, and re-layouts: 11.4 us -> none  [the longest x2 11.4 us: place(): jnp.stack(numbers)]
  transfers between devices with their start and end apart: 39 -> 42, of which waited for: 13 -> 21; matrix products, arithmetic and copies ran while one was open for 3% -> 0% of each run, Pallas kernels for 35% -> 15%
where the time goes in v2:
time: 203 us
  waiting for transfers between devices  100 us (49%)
  starting transfers between devices  58.2 us (29%)
  Pallas kernels  38.6 us (19%)
  local copies, waits for them, and re-layouts  4.23 us (2%)
    ppermute x42, waiting for transfers between devices, move(): return lax.ppermute(value, ('dp', 'mp'), route)  100 us
    ppermute x42, starting transfers between devices, move(): return lax.ppermute(value, ('dp', 'mp'), route)  58.2 us
    pallas_call x2, Pallas kernels, grad_chunk(): pl.pallas_call(functools.partial(grad_kernel, rows, span), out_shape=(hal...  17.2 us
    pallas_call x2, Pallas kernels, place(): pl.pallas_call(functools.partial(place_kernel, whence, int(aliased)), out...  7.84 us
  transfers between devices with their start and end apart: 42, of which 21 were waited for; matrix products, arithmetic and copies ran while one was open for 0% of the time, Pallas kernels for 15%

profile of v2, /device:TPU:1, one launch (start us, length us, event | category | flops | bytes accessed | tf_op | source)
XLA Modules:
  0.0 202.9 jit_solution(15780567415867102281)
XLA Ops:
  5.8 2.7 %collective-permute-start.2 = (bf16[2048,128]{1,0:T(8,128)(2,1)S(1)}, bf16[2048,128]{1,0:T(8,128)(2,1)S(1)}, u32[]{:S(2)}, u32[]{:S(2)}) collective-permute-start(bf16[2048,128]{1,0:T(8,128)(2,1)S(1)} %bitcast.21), channel_id=1, source_target_pairs={{0,2},{1,3},{2,0},{3,1},{4,6},{5,7},{6,4},{7,5},{8,10},{9,11},{10,... | collective-permute-start | bytes 1572872 | tf_op jit(solution)/shard_map/ppermute | solution.py:56
  8.5 8.9 %collective-permute-done.3.refs_4_ = bf16[2048,128]{1,0:T(8,128)(2,1)S(1)} collective-permute-done((bf16[2048,128]{1,0:T(8,128)(2,1)S(1)}, bf16[2048,128]{1,0:T(8,128)(2,1)S(1)}, u32[]{:S(2)}, u32[]{:S(2)}) %collective-permute-start.3) | collective-permute-done | bytes 524320 | tf_op jit(solution)/shard_map/ppermute | solution.py:56
  22.7 7.1 %collective-permute-done.7.refs_4_ = bf16[2048,128]{1,0:T(8,128)(2,1)} collective-permute-done((bf16[2048,128]{1,0:T(8,128)(2,1)}, bf16[2048,128]{1,0:T(8,128)(2,1)}, u32[]{:S(2)}, u32[]{:S(2)}) %collective-permute-start.7) | collective-permute-done | bytes 524320 | tf_op jit(solution)/shard_map/ppermute | solution.py:56
  32.1 8.8 %collective-permute-done.6.refs_7_ = bf16[2048,128]{1,0:T(8,128)(2,1)S(1)} collective-permute-done((bf16[2048,128]{1,0:T(8,128)(2,1)S(1)}, bf16[2048,128]{1,0:T(8,128)(2,1)S(1)}, u32[]{:S(2)}, u32[]{:S(2)}) %collective-permute-start.6) | collective-permute-done | bytes 524320 | tf_op jit(solution)/shard_map/ppermute | solution.py:56
  45.1 8.7 %grad_chunk.2 = (bf16[8,256,512]{2,1,0:T(8,128)(2,1)S(1)}, bf16[8,256,512]{2,1,0:T(8,128)(2,1)S(1)}) custom-call(s32[16]{0:T(128)S(1)} %bitcast.35, bf16[2048,128]{1,0:T(8,128)(2,1)S(1)} %bitcast.24, bf16[2048,128]{1,0:T(8,128)(2,1)S(1)} %collective-permute-done.refs_1_, bf16[2048,128]{1,0:T(8,128)(2,1)S(1)} %collective-permute-done.1.refs_2_, ...), custom_call_target="tpu_custom_call" | custom-call | flops 999999995904 | bytes 999999995904 | tf_op jit(solution)/shard_map/grad_chunk/pallas_call | solution.py:171
  63.2 10.4 %collective-permute-done.15.refs_3_ = bf16[2048,128]{1,0:T(8,128)(2,1)} collective-permute-done((bf16[2048,128]{1,0:T(8,128)(2,1)}, bf16[2048,128]{1,0:T(8,128)(2,1)}, u32[]{:S(2)}, u32[]{:S(2)}) %collective-permute-start.15) | collective-permute-done | bytes 524320 | tf_op jit(solution)/shard_map/ppermute | solution.py:56
  76.6 2.8 %collective-permute-start.11 = (bf16[2,256,512]{2,1,0:T(8,128)(2,1)}, bf16[2,256,512]{2,1,0:T(8,128)(2,1)}, u32[]{:S(2)}, u32[]{:S(2)}) collective-permute-start(bf16[2,256,512]{2,1,0:T(8,128)(2,1)} %get-tuple-element.48), channel_id=1, source_target_pairs={{0,32},{1,33},{2,34},{3,35},{4,36},{5,37},{6,38},{7,39},{8,104},{9... | collective-permute-start | bytes 1572872 | tf_op jit(solution)/shard_map/ppermute | solution.py:56
  79.4 6.7 %collective-permute-done.18.refs_7_ = bf16[2048,128]{1,0:T(8,128)(2,1)} collective-permute-done((bf16[2048,128]{1,0:T(8,128)(2,1)}, bf16[2048,128]{1,0:T(8,128)(2,1)}, u32[]{:S(2)}, u32[]{:S(2)}) %collective-permute-start.18) | collective-permute-done | bytes 524320 | tf_op jit(solution)/shard_map/ppermute | solution.py:56
  86.1 2.8 %collective-permute-start.13 = (bf16[2,256,512]{2,1,0:T(8,128)(2,1)}, bf16[2,256,512]{2,1,0:T(8,128)(2,1)}, u32[]{:S(2)}, u32[]{:S(2)}) collective-permute-start(bf16[2,256,512]{2,1,0:T(8,128)(2,1)} %get-tuple-element.50), channel_id=1, source_target_pairs={{0,64},{1,65},{2,66},{3,67},{4,68},{5,69},{6,70},{7,71},{8,72},{9,... | collective-permute-start | bytes 1572872 | tf_op jit(solution)/shard_map/ppermute | solution.py:56
  89.0 8.5 %grad_chunk.3 = (bf16[8,256,512]{2,1,0:T(8,128)(2,1)S(1)}, bf16[8,256,512]{2,1,0:T(8,128)(2,1)}) custom-call(s32[16]{0:T(128)S(1)} %bitcast.36, bf16[2048,128]{1,0:T(8,128)(2,1)} %bitcast.6.refs_0_, bf16[2048,128]{1,0:T(8,128)(2,1)} %collective-permute-done.8.refs_1_, bf16[2048,128]{1,0:T(8,128)(2,1)} %collective-permute-done.9.refs_2_, ...), custom_call_target="tpu_custom_call" | custom-call | flops 999999995904 | bytes 999999995904 | tf_op jit(solution)/shard_map/grad_chunk/pallas_call | solution.py:171
  97.5 7.7 %collective-permute-done.12.refs_2_ = bf16[2,256,512]{2,1,0:T(8,128)(2,1)} collective-permute-done((bf16[2,256,512]{2,1,0:T(8,128)(2,1)}, bf16[2,256,512]{2,1,0:T(8,128)(2,1)}, u32[]{:S(2)}, u32[]{:S(2)}) %collective-permute-start.12) | collective-permute-done | bytes 524320 | tf_op jit(solution)/shard_map/ppermute | solution.py:56
  113.3 3.3 %collective-permute-start.14 = (bf16[256,512]{1,0:T(8,128)(2,1)S(1)}, bf16[256,512]{1,0:T(8,128)(2,1)S(1)}, u32[]{:S(2)}, u32[]{:S(2)}) collective-permute-start(bf16[256,512]{1,0:T(8,128)(2,1)S(1)} %get-tuple-element.52), channel_id=1, source_target_pairs={{0,16},{1,17},{2,18},{3,19},{4,20},{5,21},{6,22},{7,23},{8,24},{9,... | collective-permute-start | bytes 786440 | tf_op jit(solution)/shard_map/ppermute | solution.py:56
  119.2 3.1 %collective-permute-start.24 = (bf16[256,512]{1,0:T(8,128)(2,1)S(1)}, bf16[256,512]{1,0:T(8,128)(2,1)S(1)}, u32[]{:S(2)}, u32[]{:S(2)}) collective-permute-start(bf16[256,512]{1,0:T(8,128)(2,1)S(1)} %bitcast.30), channel_id=1, source_target_pairs={{0,80},{1,81},{2,82},{3,83},{4,84},{5,85},{6,86},{7,87},{8,88},{9,... | collective-permute-start | bytes 786440 | tf_op jit(solution)/shard_map/ppermute | solution.py:56
  122.3 8.2 %collective-permute-done.21.refs_4_ = bf16[256,512]{1,0:T(8,128)(2,1)S(1)} collective-permute-done((bf16[256,512]{1,0:T(8,128)(2,1)S(1)}, bf16[256,512]{1,0:T(8,128)(2,1)S(1)}, u32[]{:S(2)}, u32[]{:S(2)}) %collective-permute-start.21) | collective-permute-done | bytes 262176 | tf_op jit(solution)/shard_map/ppermute | solution.py:56
  134.4 8.8 %collective-permute-done.25.refs_8_ = bf16[256,512]{1,0:T(8,128)(2,1)S(1)} collective-permute-done((bf16[256,512]{1,0:T(8,128)(2,1)S(1)}, bf16[256,512]{1,0:T(8,128)(2,1)S(1)}, u32[]{:S(2)}, u32[]{:S(2)}) %collective-permute-start.25) | collective-permute-done | bytes 262176 | tf_op jit(solution)/shard_map/ppermute | solution.py:56
  143.2 7.2 %collective-permute-done.26.refs_9_ = bf16[256,512]{1,0:T(8,128)(2,1)S(1)} collective-permute-done((bf16[256,512]{1,0:T(8,128)(2,1)S(1)}, bf16[256,512]{1,0:T(8,128)(2,1)S(1)}, u32[]{:S(2)}, u32[]{:S(2)}) %collective-permute-start.26) | collective-permute-done | bytes 262176 | tf_op jit(solution)/shard_map/ppermute | solution.py:56
  150.4 2.9 %apply_roots.1 = (bf16[512,512]{1,0:T(8,128)(2,1)}, f32[512,512]{1,0:T(8,128)S(1)}) custom-call(f32[256,512]{1,0:T(8,128)S(1)} %get-tuple-element.51.refs_0_, bf16[256,512]{1,0:T(8,128)(2,1)S(1)} %collective-permute-done.14.refs_1_, bf16[256,512]{1,0:T(8,128)(2,1)S(1)} %bitcast.41, bf16[256,512]{1,0:T(8,128)(2,1)S(1)} %collective-permute-done.20.refs_3_, ...), custom_call_target="tpu_custom_call" | custom-call | flops 999999995904 | bytes 999999995904 | tf_op jit(solution)/shard_map/apply_roots/pallas_call | solution.py:307
  157.6 3.2 %statistics.1.stats_ref = f32[2,512,512]{2,1,0:T(8,128)} custom-call(f32[512,512]{1,0:T(8,128)S(1)} %get-tuple-element.69.grad_ref, f32[2,512,512]{2,1,0:T(8,128)S(1)} %bitcast.25), custom_call_target="tpu_custom_call" | custom-call | flops 999999995904 | bytes 999999995904 | tf_op jit(solution)/shard_map/statistics/pallas_call | solution.py:328
  160.8 7.1 %collective-permute-done.28.refs_2_ = bf16[512,512]{1,0:T(8,128)(2,1)} collective-permute-done((bf16[512,512]{1,0:T(8,128)(2,1)}, bf16[512,512]{1,0:T(8,128)(2,1)}, u32[]{:S(2)}, u32[]{:S(2)}) %collective-permute-start.28) | collective-permute-done | bytes 524320 | tf_op jit(solution)/shard_map/ppermute | solution.py:56
  171.5 5.0 %collective-permute-done.30.refs_7_ = bf16[512,512]{1,0:T(8,128)(2,1)} collective-permute-done((bf16[512,512]{1,0:T(8,128)(2,1)}, bf16[512,512]{1,0:T(8,128)(2,1)}, u32[]{:S(2)}, u32[]{:S(2)}) %collective-permute-start.30) | collective-permute-done | bytes 524320 | tf_op jit(solution)/shard_map/ppermute | solution.py:56
  176.5 2.7 %collective-permute-start.31 = (bf16[512,512]{1,0:T(8,128)(2,1)}, bf16[512,512]{1,0:T(8,128)(2,1)}, u32[]{:S(2)}, u32[]{:S(2)}) collective-permute-start(bf16[512,512]{1,0:T(8,128)(2,1)} %collective-permute-done.27.refs_6_), channel_id=1, source_target_pairs={{0,32},{1,33},{2,34},{3,35},{4,36},{5,37},{6,38},{7,39},{8,104},{9... | collective-permute-start | bytes 1572872 | tf_op jit(solution)/shard_map/ppermute | solution.py:56
  179.2 3.3 %collective-permute-start.38 = (bf16[512,512]{1,0:T(8,128)(2,1)}, bf16[512,512]{1,0:T(8,128)(2,1)}, u32[]{:S(2)}, u32[]{:S(2)}) collective-permute-start(bf16[512,512]{1,0:T(8,128)(2,1)} %collective-permute-done.30.refs_7_), channel_id=1, source_target_pairs={{0,16},{1,17},{2,18},{3,19},{4,20},{5,21},{6,22},{7,23},{8,24},{9,... | collective-permute-start | bytes 1572872 | tf_op jit(solution)/shard_map/ppermute | solution.py:56
  186.1 4.1 %place.2.refs_8_ = bf16[4096,1024]{1,0:T(8,128)(2,1)} custom-call(s32[16]{0:T(128)S(1)} %bitcast.38, bf16[512,512]{1,0:T(8,128)(2,1)} %get-tuple-element.68.refs_0_, bf16[512,512]{1,0:T(8,128)(2,1)} %collective-permute-done.29.refs_1_, bf16[512,512]{1,0:T(8,128)(2,1)} %collective-permute-done.28.refs_2_, bf16[512,512]{1,0:T(8,128)(2,1)} %collective-permute-done.32.refs_3_, ...), custom_call_target="tpu_custom_call" | custom-call | flops 999999995904 | bytes 999999995904 | tf_op jit(solution)/shard_map/place/pallas_call | solution.py:417
  199.0 3.7 %place.3 = bf16[4096,1024]{1,0:T(8,128)(2,1)} custom-call(s32[16]{0:T(128)S(1)} %bitcast.39, bf16[512,512]{1,0:T(8,128)(2,1)} %collective-permute-done.31.refs_0_, bf16[512,512]{1,0:T(8,128)(2,1)S(1)} %collective-permute-done.35.refs_1_, bf16[512,512]{1,0:T(8,128)(2,1)} %collective-permute-done.36.refs_2_, ...), custom_call_target="tpu_custom_call", output_to_operand_aliasing={{}: (9, {})} | custom-call | flops 999999995904 | bytes 999999995904 | tf_op jit(solution)/shard_map/place/pallas_call | solution.py:417
  (82 shorter events, 63.5 us)
Async XLA Ops:
  19.7 21.2 %collective-permute-start.6 = (bf16[2048,128]{1,0:T(8,128)(2,1)S(1)}, bf16[2048,128]{1,0:T(8,128)(2,1)S(1)}, u32[]{:S(2)}, u32[]{:S(2)}) collective-permute-start(bf16[2048,128]{1,0:T(8,128)(2,1)S(1)} %collective-permute-done.2.refs_3_), channel_id=1, source_target_pairs={{0,4},{1,5},{2,6},{3,7},{4,0},{5,1},{6,2},{7,3},{8,12},{9,13},{10,... | collective-permute-start | bytes 1572872 | tf_op jit(solution)/shard_map/ppermute | solution.py:56
  20.0 22.0 %collective-permute-start.1 = (bf16[2048,128]{1,0:T(8,128)(2,1)S(1)}, bf16[2048,128]{1,0:T(8,128)(2,1)S(1)}, u32[]{:S(2)}, u32[]{:S(2)}) collective-permute-start(bf16[2048,128]{1,0:T(8,128)(2,1)S(1)} %bitcast.22), channel_id=1, source_target_pairs={{0,3},{1,0},{2,1},{3,2},{4,7},{5,4},{6,5},{7,6},{8,9},{9,10},{10,1... | collective-permute-start | bytes 1572872 | tf_op jit(solution)/shard_map/ppermute | solution.py:56
  21.1 22.5 %collective-permute-start = (bf16[2048,128]{1,0:T(8,128)(2,1)S(1)}, bf16[2048,128]{1,0:T(8,128)(2,1)S(1)}, u32[]{:S(2)}, u32[]{:S(2)}) collective-permute-start(bf16[2048,128]{1,0:T(8,128)(2,1)S(1)} %bitcast.23), channel_id=1, source_target_pairs={{0,1},{1,2},{2,3},{3,0},{4,5},{5,6},{6,7},{7,4},{8,11},{9,8},{10,9... | collective-permute-start | bytes 1572872 | tf_op jit(solution)/shard_map/ppermute | solution.py:56
  22.7 21.0 %collective-permute-start.5 = (bf16[2048,128]{1,0:T(8,128)(2,1)S(1)}, bf16[2048,128]{1,0:T(8,128)(2,1)S(1)}, u32[]{:S(2)}, u32[]{:S(2)}) collective-permute-start(bf16[2048,128]{1,0:T(8,128)(2,1)S(1)} %collective-permute-done.3.refs_4_), channel_id=1, source_target_pairs={{0,3},{1,0},{2,1},{3,2},{4,7},{5,4},{6,5},{7,6},{8,9},{9,10},{10,1... | collective-permute-start | bytes 1572872 | tf_op jit(solution)/shard_map/ppermute | solution.py:56
  29.9 15.2 %collective-permute-start.4 = (bf16[2048,128]{1,0:T(8,128)(2,1)S(1)}, bf16[2048,128]{1,0:T(8,128)(2,1)S(1)}, u32[]{:S(2)}, u32[]{:S(2)}) collective-permute-start(bf16[2048,128]{1,0:T(8,128)(2,1)S(1)} %collective-permute-done.3.refs_4_), channel_id=1, source_target_pairs={{0,1},{1,2},{2,3},{3,0},{4,5},{5,6},{6,7},{7,4},{8,11},{9,8},{10,9... | collective-permute-start | bytes 1572872 | tf_op jit(solution)/shard_map/ppermute | solution.py:56
  56.4 18.3 %collective-permute-start.10 = (bf16[8,256,512]{2,1,0:T(8,128)(2,1)S(1)}, bf16[8,256,512]{2,1,0:T(8,128)(2,1)S(1)}, u32[]{:S(2)}, u32[]{:S(2)}) collective-permute-start(bf16[8,256,512]{2,1,0:T(8,128)(2,1)S(1)} %get-tuple-element.46), channel_id=1, source_target_pairs={{0,8},{1,9},{2,10},{3,11},{4,12},{5,13},{6,14},{7,15},{8,0},{9,1},... | collective-permute-start | bytes 6291464 | tf_op jit(solution)/shard_map/ppermute | solution.py:56
  58.1 15.4 %collective-permute-start.15 = (bf16[2048,128]{1,0:T(8,128)(2,1)}, bf16[2048,128]{1,0:T(8,128)(2,1)}, u32[]{:S(2)}, u32[]{:S(2)}) collective-permute-start(bf16[2048,128]{1,0:T(8,128)(2,1)} %bitcast.6.refs_0_), channel_id=1, source_target_pairs={{0,2},{1,3},{2,0},{3,1},{4,6},{5,7},{6,4},{7,5},{8,10},{9,11},{10,... | collective-permute-start | bytes 1572872 | tf_op jit(solution)/shard_map/ppermute | solution.py:56
  60.5 28.5 %collective-permute-start.17 = (bf16[2048,128]{1,0:T(8,128)(2,1)}, bf16[2048,128]{1,0:T(8,128)(2,1)}, u32[]{:S(2)}, u32[]{:S(2)}) collective-permute-start(bf16[2048,128]{1,0:T(8,128)(2,1)} %collective-permute-done.7.refs_4_), channel_id=1, source_target_pairs={{0,3},{1,0},{2,1},{3,2},{4,7},{5,4},{6,5},{7,6},{8,9},{9,10},{10,1... | collective-permute-start | bytes 1572872 | tf_op jit(solution)/shard_map/ppermute | solution.py:56
  61.4 27.6 %collective-permute-start.16 = (bf16[2048,128]{1,0:T(8,128)(2,1)}, bf16[2048,128]{1,0:T(8,128)(2,1)}, u32[]{:S(2)}, u32[]{:S(2)}) collective-permute-start(bf16[2048,128]{1,0:T(8,128)(2,1)} %collective-permute-done.7.refs_4_), channel_id=1, source_target_pairs={{0,1},{1,2},{2,3},{3,0},{4,5},{5,6},{6,7},{7,4},{8,11},{9,8},{10,9... | collective-permute-start | bytes 1572872 | tf_op jit(solution)/shard_map/ppermute | solution.py:56
  76.6 20.8 %collective-permute-start.11 = (bf16[2,256,512]{2,1,0:T(8,128)(2,1)}, bf16[2,256,512]{2,1,0:T(8,128)(2,1)}, u32[]{:S(2)}, u32[]{:S(2)}) collective-permute-start(bf16[2,256,512]{2,1,0:T(8,128)(2,1)} %get-tuple-element.48), channel_id=1, source_target_pairs={{0,32},{1,33},{2,34},{3,35},{4,36},{5,37},{6,38},{7,39},{8,104},{9... | collective-permute-start | bytes 1572872 | tf_op jit(solution)/shard_map/ppermute | solution.py:56
  79.4 25.7 %collective-permute-start.12 = (bf16[2,256,512]{2,1,0:T(8,128)(2,1)}, bf16[2,256,512]{2,1,0:T(8,128)(2,1)}, u32[]{:S(2)}, u32[]{:S(2)}) collective-permute-start(bf16[2,256,512]{2,1,0:T(8,128)(2,1)} %get-tuple-element.49), channel_id=1, source_target_pairs={{0,96},{1,97},{2,98},{3,99},{4,100},{5,101},{6,102},{7,103},{8,40}... | collective-permute-start | bytes 1572872 | tf_op jit(solution)/shard_map/ppermute | solution.py:56
  86.1 19.0 %collective-permute-start.13 = (bf16[2,256,512]{2,1,0:T(8,128)(2,1)}, bf16[2,256,512]{2,1,0:T(8,128)(2,1)}, u32[]{:S(2)}, u32[]{:S(2)}) collective-permute-start(bf16[2,256,512]{2,1,0:T(8,128)(2,1)} %get-tuple-element.50), channel_id=1, source_target_pairs={{0,64},{1,65},{2,66},{3,67},{4,68},{5,69},{6,70},{7,71},{8,72},{9,... | collective-permute-start | bytes 1572872 | tf_op jit(solution)/shard_map/ppermute | solution.py:56
  112.7 17.8 %collective-permute-start.21 = (bf16[256,512]{1,0:T(8,128)(2,1)S(1)}, bf16[256,512]{1,0:T(8,128)(2,1)S(1)}, u32[]{:S(2)}, u32[]{:S(2)}) collective-permute-start(bf16[256,512]{1,0:T(8,128)(2,1)S(1)} %bitcast.33), channel_id=1, source_target_pairs={{0,96},{1,97},{2,98},{3,99},{4,100},{5,101},{6,102},{7,103},{8,40}... | collective-permute-start | bytes 786440 | tf_op jit(solution)/shard_map/ppermute | solution.py:56
  113.3 19.7 %collective-permute-start.14 = (bf16[256,512]{1,0:T(8,128)(2,1)S(1)}, bf16[256,512]{1,0:T(8,128)(2,1)S(1)}, u32[]{:S(2)}, u32[]{:S(2)}) collective-permute-start(bf16[256,512]{1,0:T(8,128)(2,1)S(1)} %get-tuple-element.52), channel_id=1, source_target_pairs={{0,16},{1,17},{2,18},{3,19},{4,20},{5,21},{6,22},{7,23},{8,24},{9,... | collective-permute-start | bytes 786440 | tf_op jit(solution)/shard_map/ppermute | solution.py:56
  116.6 17.8 %collective-permute-start.22 = (bf16[256,512]{1,0:T(8,128)(2,1)S(1)}, bf16[256,512]{1,0:T(8,128)(2,1)S(1)}, u32[]{:S(2)}, u32[]{:S(2)}) collective-permute-start(bf16[256,512]{1,0:T(8,128)(2,1)S(1)} %bitcast.32), channel_id=1, source_target_pairs={{0,64},{1,65},{2,66},{3,67},{4,68},{5,69},{6,70},{7,71},{8,72},{9,... | collective-permute-start | bytes 786440 | tf_op jit(solution)/shard_map/ppermute | solution.py:56
  117.8 16.6 %collective-permute-start.23 = (bf16[256,512]{1,0:T(8,128)(2,1)S(1)}, bf16[256,512]{1,0:T(8,128)(2,1)S(1)}, u32[]{:S(2)}, u32[]{:S(2)}) collective-permute-start(bf16[256,512]{1,0:T(8,128)(2,1)S(1)} %bitcast.31), channel_id=1, source_target_pairs={{0,16},{1,17},{2,18},{3,19},{4,20},{5,21},{6,22},{7,23},{8,24},{9,... | collective-permute-start | bytes 786440 | tf_op jit(solution)/shard_map/ppermute | solution.py:56
  119.2 15.2 %collective-permute-start.24 = (bf16[256,512]{1,0:T(8,128)(2,1)S(1)}, bf16[256,512]{1,0:T(8,128)(2,1)S(1)}, u32[]{:S(2)}, u32[]{:S(2)}) collective-permute-start(bf16[256,512]{1,0:T(8,128)(2,1)S(1)} %bitcast.30), channel_id=1, source_target_pairs={{0,80},{1,81},{2,82},{3,83},{4,84},{5,85},{6,86},{7,87},{8,88},{9,... | collective-permute-start | bytes 786440 | tf_op jit(solution)/shard_map/ppermute | solution.py:56
  132.9 17.5 %collective-permute-start.26 = (bf16[256,512]{1,0:T(8,128)(2,1)S(1)}, bf16[256,512]{1,0:T(8,128)(2,1)S(1)}, u32[]{:S(2)}, u32[]{:S(2)}) collective-permute-start(bf16[256,512]{1,0:T(8,128)(2,1)S(1)} %bitcast.28), channel_id=1, source_target_pairs={{0,112},{1,113},{2,114},{3,115},{4,116},{5,117},{6,118},{7,119},{8... | collective-permute-start | bytes 786440 | tf_op jit(solution)/shard_map/ppermute | solution.py:56
  153.3 16.6 %collective-permute-start.33 = (bf16[512,512]{1,0:T(8,128)(2,1)}, bf16[512,512]{1,0:T(8,128)(2,1)}, u32[]{:S(2)}, u32[]{:S(2)}) collective-permute-start(bf16[512,512]{1,0:T(8,128)(2,1)} %get-tuple-element.68.refs_0_), channel_id=1, source_target_pairs={{0,96},{1,97},{2,98},{3,99},{4,100},{5,101},{6,102},{7,103},{8,40}... | collective-permute-start | bytes 1572872 | tf_op jit(solution)/shard_map/ppermute | solution.py:56
  155.9 15.6 %collective-permute-start.27 = (bf16[512,512]{1,0:T(8,128)(2,1)}, bf16[512,512]{1,0:T(8,128)(2,1)}, u32[]{:S(2)}, u32[]{:S(2)}) collective-permute-start(bf16[512,512]{1,0:T(8,128)(2,1)} %get-tuple-element.68.refs_0_), channel_id=1, source_target_pairs={{0,16},{1,17},{2,18},{3,19},{4,20},{5,21},{6,22},{7,23},{8,24},{9,... | collective-permute-start | bytes 1572872 | tf_op jit(solution)/shard_map/ppermute | solution.py:56
  169.8 16.3 %collective-permute-start.32 = (bf16[512,512]{1,0:T(8,128)(2,1)}, bf16[512,512]{1,0:T(8,128)(2,1)}, u32[]{:S(2)}, u32[]{:S(2)}) collective-permute-start(bf16[512,512]{1,0:T(8,128)(2,1)} %collective-permute-done.28.refs_2_), channel_id=1, source_target_pairs={{0,8},{1,9},{2,10},{3,11},{4,12},{5,13},{6,14},{7,15},{8,0},{9,1},... | collective-permute-start | bytes 1572872 | tf_op jit(solution)/shard_map/ppermute | solution.py:56
  169.9 16.2 %collective-permute-start.34 = (bf16[512,512]{1,0:T(8,128)(2,1)}, bf16[512,512]{1,0:T(8,128)(2,1)}, u32[]{:S(2)}, u32[]{:S(2)}) collective-permute-start(bf16[512,512]{1,0:T(8,128)(2,1)} %collective-permute-done.33.refs_4_), channel_id=1, source_target_pairs={{0,8},{1,9},{2,10},{3,11},{4,12},{5,13},{6,14},{7,15},{8,0},{9,1},... | collective-permute-start | bytes 1572872 | tf_op jit(solution)/shard_map/ppermute | solution.py:56
  176.5 16.5 %collective-permute-start.36 = (bf16[512,512]{1,0:T(8,128)(2,1)}, bf16[512,512]{1,0:T(8,128)(2,1)}, u32[]{:S(2)}, u32[]{:S(2)}) collective-permute-start(bf16[512,512]{1,0:T(8,128)(2,1)} %collective-permute-done.27.refs_6_), channel_id=1, source_target_pairs={{0,96},{1,97},{2,98},{3,99},{4,100},{5,101},{6,102},{7,103},{8,40}... | collective-permute-start | bytes 1572872 | tf_op jit(solution)/shard_map/ppermute | solution.py:56
  176.5 16.5 %collective-permute-start.31 = (bf16[512,512]{1,0:T(8,128)(2,1)}, bf16[512,512]{1,0:T(8,128)(2,1)}, u32[]{:S(2)}, u32[]{:S(2)}) collective-permute-start(bf16[512,512]{1,0:T(8,128)(2,1)} %collective-permute-done.27.refs_6_), channel_id=1, source_target_pairs={{0,32},{1,33},{2,34},{3,35},{4,36},{5,37},{6,38},{7,39},{8,104},{9... | collective-permute-start | bytes 1572872 | tf_op jit(solution)/shard_map/ppermute | solution.py:56
  (23 other events, 308.6 us)

commit v3 on v2

--- a/solution.py
+++ b/solution.py
@@ -56,8 +56,8 @@
     return lax.ppermute(value, ("dp", "mp"), route)
 
 
-def cost(flops, moved):
-    return pl.CostEstimate(flops=10**12, bytes_accessed=10**12, transcendentals=0)
+def cost(micros):
+    return pl.CostEstimate(flops=int(micros * 1.15e9), bytes_accessed=1024, transcendentals=0)
 
 
 PARAMS = pltpu.CompilerParams(vmem_limit_bytes=16 * MIB)
@@ -182,7 +182,7 @@
             pltpu.SemaphoreType.DMA((BLOCKS,)),
         ],
         compiler_params=PARAMS,
-        cost_estimate=cost(2 * tokens * cols * rows * ROW_BLK, 2 * 5 * MIB),
+        cost_estimate=cost(rows / 30),
         name="grad_chunk",
     )(slot_of, *pieces, og)
 
@@ -230,7 +230,7 @@
         out_specs=(ANYWHERE,) * count,
         scratch_shapes=[held] * 3 + [pltpu.SemaphoreType.DMA((Y * ZH,))] * 3,
         compiler_params=PARAMS,
-        cost_estimate=cost(MIB, keep.size * 6),
+        cost_estimate=cost(1.9),
         name="chip_sum",
     )(keep, received)
 
@@ -282,7 +282,7 @@
             pltpu.SemaphoreType.DMA((ZH,)),
         ],
         compiler_params=PARAMS,
-        cost_estimate=cost(MIB, rows * BLOCK * 22),
+        cost_estimate=cost(1.8),
         name="y_sum",
     )(*parts)
 
@@ -313,7 +313,7 @@
         in_specs=[WHOLE] * (sum(counts) + 1),
         out_specs=(WHOLE, WHOLE),
         compiler_params=pltpu.CompilerParams(vmem_limit_bytes=16 * MIB),
-        cost_estimate=cost(6 * 2 * BLOCK**3, 5 * MIB),
+        cost_estimate=cost(2.8),
         name="apply_roots",
     )(*[term for group in terms for term in group], roots)
 
@@ -331,7 +331,7 @@
         in_specs=[WHOLE] * 2,
         out_specs=WHOLE,
         compiler_params=PARAMS,
-        cost_estimate=cost(6 * 2 * BLOCK**3, 5 * MIB),
+        cost_estimate=cost(3.2),
         name="statistics",
     )(grad, stats)
 
@@ -377,7 +377,7 @@
         in_specs=[SCALARS, SCALARS, WHOLE, WHOLE],
         out_specs=WHOLE,
         compiler_params=PARAMS,
-        cost_estimate=cost(16 * 2 * BLOCK**3, 6 * MIB),
+        cost_estimate=cost(4.0),
         name="roots",
     )(slot_of, phase, stats, roots)
 
@@ -426,7 +426,7 @@
         ],
         input_output_aliases={count + 1: 0} if aliased else {},
         compiler_params=PARAMS,
-        cost_estimate=cost(0, count * MIB),
+        cost_estimate=cost(3.7),
         name="place",
     )(slot_of, *blocks, *([into] if aliased else []))
 
@@ -451,18 +451,19 @@
     near_a, back_a = move(owns[0], X_NEAR), move(owns[0], X_BACK)
     across_b = move(after(owns[1], across_a), ZL_SWAP)
     rest_a = [move(across_a, X_NEAR), move(across_a, X_BACK), move(far_a, ZL_SWAP)]
-    rest_a[2] = after(rest_a[2], across_b)
     own_b = after(owns[1], far_a)
-    far_b, near_b, back_b = move(own_b, X_FAR), move(own_b, X_NEAR), move(own_b, X_BACK)
+    near_b, back_b = move(own_b, X_NEAR), move(own_b, X_BACK)
 
     pieces = [owns[0], near_a, back_a, far_a, across_a, *rest_a]
     keep_a, send_a = grad_chunk(pieces, slot_of, out_grad, CHUNKS[0])
-    swapped_a = move(after(send_a, near_b, back_b), C_SWAP)
+    swapped_a = move(after(send_a, near_b, back_b, across_b), C_SWAP)
     across_b = after(across_b, keep_a)
-    rest_b = [move(across_b, X_NEAR), move(across_b, X_BACK), move(far_b, ZL_SWAP)]
+    far_b = move(after(near_b, keep_a), X_NEAR)
     mine, *to = chip_sum(keep_a, swapped_a, True)
+    rest_b = [move(across_b, X_NEAR), move(across_b, X_BACK), move(after(far_b, mine), ZL_SWAP)]
     parts = [mine, move(to[0], Y_NEAR), move(to[1], Y_BACK), move(to[2], Y_FAR)]
 
+    rest_b[0] = after(rest_b[0], parts[1], parts[2])
     pieces = [owns[1], near_b, back_b, far_b, across_b, *rest_b]
     keep_b, send_b = grad_chunk(pieces, slot_of, out_grad, CHUNKS[1])
     swapped_b = move(after(send_b, *parts[1:]), C_SWAP)
@@ -471,7 +472,7 @@
     to = [part[0] for part in to]
     near, back, far = move(to[0], Y_NEAR), move(to[1], Y_BACK), move(to[2], Y_FAR)
     terms_b = [mine[0], near, back, far, move(to[3], ZH_SWAP), move(to[6], Y_FAR_Z)]
-    terms_b += [move(after(to[4], near), Y_NEAR_Z), move(after(to[5], back), Y_BACK_Z)]
+    terms_b += [move(to[4], Y_NEAR_Z), move(to[5], Y_BACK_Z)]
     terms_a = [keep_a, move(send_a, ZH_SWAP)]
 
     own, grad = apply_roots([terms_a, terms_b], roots)

time: 203 us -> 184 us (0.906)
  waiting for transfers between devices: 100 us -> 78.8 us
  starting transfers between devices: 58.2 us -> 62.4 us
  local copies, waits for them, and re-layouts: 4.23 us -> 1.85 us
    ppermute x42, waiting for transfers between devices: 100 us -> 78.8 us  [move(): return lax.ppermute(value, ('dp', 'mp'), route)]
    pallas_call x1, Pallas kernels: 2.02 us -> 7.61 us  [roots_of(): pl.pallas_call(roots_kernel, out_shape=jax.ShapeDtypeStruct(stats.shape,...]
    ppermute x42, starting transfers between devices: 58.2 us -> 62.4 us  [move(): return lax.ppermute(value, ('dp', 'mp'), route)]
  transfers between devices with their start and end apart: 42 -> 42, of which waited for: 21 -> 18; matrix products, arithmetic and copies ran while one was open for 0% -> 0% of each run, Pallas kernels for 15% -> 19%
where the time goes in v3:
time: 184 us
  waiting for transfers between devices  78.8 us (43%)
  starting transfers between devices  62.4 us (34%)
  Pallas kernels  39.3 us (21%)
  local copies, waits for them, and re-layouts  1.85 us (1%)
    ppermute x42, waiting for transfers between devices, move(): return lax.ppermute(value, ('dp', 'mp'), route)  78.8 us
    ppermute x42, starting transfers between devices, move(): return lax.ppermute(value, ('dp', 'mp'), route)  62.4 us
    pallas_call x2, Pallas kernels, grad_chunk(): pl.pallas_call(functools.partial(grad_kernel, rows, span), out_shape=(hal...  17.5 us
    pallas_call x1, Pallas kernels, roots_of(): pl.pallas_call(roots_kernel, out_shape=jax.ShapeDtypeStruct(stats.shape,...  7.61 us
    pallas_call x2, Pallas kernels, place(): pl.pallas_call(functools.partial(place_kernel, whence, int(aliased)), out...  6.02 us
  transfers between devices with their start and end apart: 42, of which 18 were waited for; matrix products, arithmetic and copies ran while one was open for 0% of the time, Pallas kernels for 19%

profile of v3, /device:TPU:1, one launch (start us, length us, event | category | flops | bytes accessed | tf_op | source)
XLA Modules:
  0.0 184.0 jit_solution(3534072678786736599)
XLA Ops:
  10.5 6.2 %collective-permute-done.3.refs_4_ = bf16[2048,128]{1,0:T(8,128)(2,1)S(1)} collective-permute-done((bf16[2048,128]{1,0:T(8,128)(2,1)S(1)}, bf16[2048,128]{1,0:T(8,128)(2,1)S(1)}, u32[]{:S(2)}, u32[]{:S(2)}) %collective-permute-start.3) | collective-permute-done | bytes 524320 | tf_op jit(solution)/shard_map/ppermute | solution.py:56
  20.5 11.1 %collective-permute-done.1.refs_2_ = bf16[2048,128]{1,0:T(8,128)(2,1)S(1)} collective-permute-done((bf16[2048,128]{1,0:T(8,128)(2,1)S(1)}, bf16[2048,128]{1,0:T(8,128)(2,1)S(1)}, u32[]{:S(2)}, u32[]{:S(2)}) %collective-permute-start.1) | collective-permute-done | bytes 524320 | tf_op jit(solution)/shard_map/ppermute | solution.py:56
  34.3 8.6 %collective-permute-done.5.refs_6_ = bf16[2048,128]{1,0:T(8,128)(2,1)S(1)} collective-permute-done((bf16[2048,128]{1,0:T(8,128)(2,1)S(1)}, bf16[2048,128]{1,0:T(8,128)(2,1)S(1)}, u32[]{:S(2)}, u32[]{:S(2)}) %collective-permute-start.5) | collective-permute-done | bytes 524320 | tf_op jit(solution)/shard_map/ppermute | solution.py:56
  43.0 8.8 %grad_chunk.2 = (bf16[8,256,512]{2,1,0:T(8,128)(2,1)S(1)}, bf16[8,256,512]{2,1,0:T(8,128)(2,1)S(1)}) custom-call(s32[16]{0:T(128)S(1)} %bitcast.29, bf16[2048,128]{1,0:T(8,128)(2,1)S(1)} %bitcast.28, bf16[2048,128]{1,0:T(8,128)(2,1)S(1)} %collective-permute-done.refs_1_, bf16[2048,128]{1,0:T(8,128)(2,1)S(1)} %collective-permute-done.1.refs_2_, ...), custom_call_target="tpu_custom_call" | custom-call | flops 9813332992 | bytes 1024 | tf_op jit(solution)/shard_map/grad_chunk/pallas_call | solution.py:171
  54.2 3.0 %collective-permute-start.10 = (bf16[8,256,512]{2,1,0:T(8,128)(2,1)S(1)}, bf16[8,256,512]{2,1,0:T(8,128)(2,1)S(1)}, u32[]{:S(2)}, u32[]{:S(2)}) collective-permute-start(bf16[8,256,512]{2,1,0:T(8,128)(2,1)S(1)} %get-tuple-element.45), channel_id=1, source_target_pairs={{0,8},{1,9},{2,10},{3,11},{4,12},{5,13},{6,14},{7,15},{8,0},{9,1},... | collective-permute-start | bytes 6291464 | tf_op jit(solution)/shard_map/ppermute | solution.py:56
  62.2 2.8 %collective-permute-start.11 = (bf16[2,256,512]{2,1,0:T(8,128)(2,1)S(1)}, bf16[2,256,512]{2,1,0:T(8,128)(2,1)S(1)}, u32[]{:S(2)}, u32[]{:S(2)}) collective-permute-start(bf16[2,256,512]{2,1,0:T(8,128)(2,1)S(1)} %get-tuple-element.47), channel_id=1, source_target_pairs={{0,32},{1,33},{2,34},{3,35},{4,36},{5,37},{6,38},{7,39},{8,104},{9... | collective-permute-start | bytes 1572872 | tf_op jit(solution)/shard_map/ppermute | solution.py:56
  65.0 5.4 %collective-permute-done.15.refs_3_ = bf16[2048,128]{1,0:T(8,128)(2,1)S(1)} collective-permute-done((bf16[2048,128]{1,0:T(8,128)(2,1)S(1)}, bf16[2048,128]{1,0:T(8,128)(2,1)S(1)}, u32[]{:S(2)}, u32[]{:S(2)}) %collective-permute-start.15) | collective-permute-done | bytes 524320 | tf_op jit(solution)/shard_map/ppermute | solution.py:56
  70.4 6.4 %collective-permute-done.16.refs_5_ = bf16[2048,128]{1,0:T(8,128)(2,1)S(1)} collective-permute-done((bf16[2048,128]{1,0:T(8,128)(2,1)S(1)}, bf16[2048,128]{1,0:T(8,128)(2,1)S(1)}, u32[]{:S(2)}, u32[]{:S(2)}) %collective-permute-start.16) | collective-permute-done | bytes 524320 | tf_op jit(solution)/shard_map/ppermute | solution.py:56
  76.8 2.9 %collective-permute-start.13 = (bf16[2,256,512]{2,1,0:T(8,128)(2,1)S(1)}, bf16[2,256,512]{2,1,0:T(8,128)(2,1)S(1)}, u32[]{:S(2)}, u32[]{:S(2)}) collective-permute-start(bf16[2,256,512]{2,1,0:T(8,128)(2,1)S(1)} %get-tuple-element.49), channel_id=1, source_target_pairs={{0,64},{1,65},{2,66},{3,67},{4,68},{5,69},{6,70},{7,71},{8,72},{9,... | collective-permute-start | bytes 1572872 | tf_op jit(solution)/shard_map/ppermute | solution.py:56
  81.5 8.8 %grad_chunk.3 = (bf16[8,256,512]{2,1,0:T(8,128)(2,1)S(1)}, bf16[8,256,512]{2,1,0:T(8,128)(2,1)S(1)}) custom-call(s32[16]{0:T(128)S(1)} %bitcast.30, bf16[2048,128]{1,0:T(8,128)(2,1)S(1)} %bitcast.23, bf16[2048,128]{1,0:T(8,128)(2,1)S(1)} %collective-permute-done.7.refs_1_, bf16[2048,128]{1,0:T(8,128)(2,1)S(1)} %collective-permute-done.8.refs_2_, ...), custom_call_target="tpu_custom_call" | custom-call | flops 9813332992 | bytes 1024 | tf_op jit(solution)/shard_map/grad_chunk/pallas_call | solution.py:171
  90.2 3.4 %collective-permute-start.19 = (bf16[8,256,512]{2,1,0:T(8,128)(2,1)S(1)}, bf16[8,256,512]{2,1,0:T(8,128)(2,1)S(1)}, u32[]{:S(2)}, u32[]{:S(2)}) collective-permute-start(bf16[8,256,512]{2,1,0:T(8,128)(2,1)S(1)} %get-tuple-element.58), channel_id=1, source_target_pairs={{0,8},{1,9},{2,10},{3,11},{4,12},{5,13},{6,14},{7,15},{8,0},{9,1},... | collective-permute-start | bytes 6291464 | tf_op jit(solution)/shard_map/ppermute | solution.py:56
  94.2 3.4 %collective-permute-start.14 = (bf16[256,512]{1,0:T(8,128)(2,1)S(1)}, bf16[256,512]{1,0:T(8,128)(2,1)S(1)}, u32[]{:S(2)}, u32[]{:S(2)}) collective-permute-start(bf16[256,512]{1,0:T(8,128)(2,1)S(1)} %get-tuple-element.51), channel_id=1, source_target_pairs={{0,16},{1,17},{2,18},{3,19},{4,20},{5,21},{6,22},{7,23},{8,24},{9,... | collective-permute-start | bytes 786440 | tf_op jit(solution)/shard_map/ppermute | solution.py:56
  103.2 3.1 %collective-permute-start.23 = (bf16[256,512]{1,0:T(8,128)(2,1)S(1)}, bf16[256,512]{1,0:T(8,128)(2,1)S(1)}, u32[]{:S(2)}, u32[]{:S(2)}) collective-permute-start(bf16[256,512]{1,0:T(8,128)(2,1)S(1)} %bitcast.40), channel_id=1, source_target_pairs={{0,16},{1,17},{2,18},{3,19},{4,20},{5,21},{6,22},{7,23},{8,24},{9,... | collective-permute-start | bytes 786440 | tf_op jit(solution)/shard_map/ppermute | solution.py:56
  106.3 3.2 %collective-permute-start.24 = (bf16[256,512]{1,0:T(8,128)(2,1)S(1)}, bf16[256,512]{1,0:T(8,128)(2,1)S(1)}, u32[]{:S(2)}, u32[]{:S(2)}) collective-permute-start(bf16[256,512]{1,0:T(8,128)(2,1)S(1)} %bitcast.39), channel_id=1, source_target_pairs={{0,80},{1,81},{2,82},{3,83},{4,84},{5,85},{6,86},{7,87},{8,88},{9,... | collective-permute-start | bytes 786440 | tf_op jit(solution)/shard_map/ppermute | solution.py:56
  109.6 8.2 %collective-permute-done.20.refs_3_ = bf16[256,512]{1,0:T(8,128)(2,1)S(1)} collective-permute-done((bf16[256,512]{1,0:T(8,128)(2,1)S(1)}, bf16[256,512]{1,0:T(8,128)(2,1)S(1)}, u32[]{:S(2)}, u32[]{:S(2)}) %collective-permute-start.20) | collective-permute-done | bytes 262176 | tf_op jit(solution)/shard_map/ppermute | solution.py:56
  117.8 6.3 %collective-permute-start.25 = (bf16[256,512]{1,0:T(8,128)(2,1)S(1)}, bf16[256,512]{1,0:T(8,128)(2,1)S(1)}, u32[]{:S(2)}, u32[]{:S(2)}) collective-permute-start(bf16[256,512]{1,0:T(8,128)(2,1)S(1)} %bitcast.38), channel_id=1, source_target_pairs={{0,48},{1,49},{2,50},{3,51},{4,52},{5,53},{6,54},{7,55},{8,120},{9... | collective-permute-start | bytes 786440 | tf_op jit(solution)/shard_map/ppermute | solution.py:56
  124.7 6.6 %collective-permute-done.25.refs_8_ = bf16[256,512]{1,0:T(8,128)(2,1)S(1)} collective-permute-done((bf16[256,512]{1,0:T(8,128)(2,1)S(1)}, bf16[256,512]{1,0:T(8,128)(2,1)S(1)}, u32[]{:S(2)}, u32[]{:S(2)}) %collective-permute-start.25) | collective-permute-done | bytes 262176 | tf_op jit(solution)/shard_map/ppermute | solution.py:56
  131.3 3.8 %collective-permute-done.26.refs_9_ = bf16[256,512]{1,0:T(8,128)(2,1)S(1)} collective-permute-done((bf16[256,512]{1,0:T(8,128)(2,1)S(1)}, bf16[256,512]{1,0:T(8,128)(2,1)S(1)}, u32[]{:S(2)}, u32[]{:S(2)}) %collective-permute-start.26) | collective-permute-done | bytes 262176 | tf_op jit(solution)/shard_map/ppermute | solution.py:56
  140.5 3.2 %statistics.1.stats_ref = f32[2,512,512]{2,1,0:T(8,128)} custom-call(f32[512,512]{1,0:T(8,128)S(1)} %get-tuple-element.69.grad_ref, f32[2,512,512]{2,1,0:T(8,128)S(1)} %bitcast.34), custom_call_target="tpu_custom_call" | custom-call | flops 3680000000 | bytes 1024 | tf_op jit(solution)/shard_map/statistics/pallas_call | solution.py:328
  143.7 7.3 %collective-permute-done.28.refs_2_ = bf16[512,512]{1,0:T(8,128)(2,1)S(1)} collective-permute-done((bf16[512,512]{1,0:T(8,128)(2,1)S(1)}, bf16[512,512]{1,0:T(8,128)(2,1)S(1)}, u32[]{:S(2)}, u32[]{:S(2)}) %collective-permute-start.28) | collective-permute-done | bytes 524320 | tf_op jit(solution)/shard_map/ppermute | solution.py:56
  154.6 4.7 %collective-permute-done.30.refs_7_ = bf16[512,512]{1,0:T(8,128)(2,1)S(1)} collective-permute-done((bf16[512,512]{1,0:T(8,128)(2,1)S(1)}, bf16[512,512]{1,0:T(8,128)(2,1)S(1)}, u32[]{:S(2)}, u32[]{:S(2)}) %collective-permute-start.30) | collective-permute-done | bytes 524320 | tf_op jit(solution)/shard_map/ppermute | solution.py:56
  164.0 3.0 %place.2.refs_8_ = bf16[4096,1024]{1,0:T(8,128)(2,1)} custom-call(s32[16]{0:T(128)S(1)} %bitcast.31, bf16[512,512]{1,0:T(8,128)(2,1)S(1)} %get-tuple-element.68.refs_0_, bf16[512,512]{1,0:T(8,128)(2,1)S(1)} %collective-permute-done.29.refs_1_, bf16[512,512]{1,0:T(8,128)(2,1)S(1)} %collective-permute-done.28.refs_2_, ...), custom_call_target="tpu_custom_call" | custom-call | flops 4255000064 | bytes 1024 | tf_op jit(solution)/shard_map/place/pallas_call | solution.py:417
  167.1 7.6 %roots.1 = f32[2,512,512]{2,1,0:T(8,128)} custom-call(s32[16]{0:T(128)S(1)} %bitcast.32, s32[1]{0:T(128)S(6)} %copy.14.phase, f32[2,512,512]{2,1,0:T(8,128)S(1)} %copy-done.4, f32[2,512,512]{2,1,0:T(8,128)S(1)} %bitcast.36), custom_call_target="tpu_custom_call" | custom-call | flops 4600000000 | bytes 1024 | tf_op jit(solution)/shard_map/roots/pallas_call | solution.py:374
  180.8 3.0 %place.3 = bf16[4096,1024]{1,0:T(8,128)(2,1)} custom-call(s32[16]{0:T(128)S(1)} %bitcast.33, bf16[512,512]{1,0:T(8,128)(2,1)S(1)} %collective-permute-done.31.refs_0_, bf16[512,512]{1,0:T(8,128)(2,1)S(1)} %collective-permute-done.35.refs_1_, bf16[512,512]{1,0:T(8,128)(2,1)S(1)} %collective-permute-done.36.refs_2_, ...), custom_call_target="tpu_custom_call", output_to_operand_aliasing={{}: (9, {})} | custom-call | flops 4255000064 | bytes 1024 | tf_op jit(solution)/shard_map/place/pallas_call | solution.py:417
  (82 shorter events, 51.7 us)
Async XLA Ops:
  2.5 14.2 %collective-permute-start.3 = (bf16[2048,128]{1,0:T(8,128)(2,1)S(1)}, bf16[2048,128]{1,0:T(8,128)(2,1)S(1)}, u32[]{:S(2)}, u32[]{:S(2)}) collective-permute-start(bf16[2048,128]{1,0:T(8,128)(2,1)S(1)} %bitcast.24), channel_id=1, source_target_pairs={{0,4},{1,5},{2,6},{3,7},{4,0},{5,1},{6,2},{7,3},{8,12},{9,13},{10,... | collective-permute-start | bytes 1572872 | tf_op jit(solution)/shard_map/ppermute | solution.py:56
  5.0 14.3 %collective-permute-start.2 = (bf16[2048,128]{1,0:T(8,128)(2,1)S(1)}, bf16[2048,128]{1,0:T(8,128)(2,1)S(1)}, u32[]{:S(2)}, u32[]{:S(2)}) collective-permute-start(bf16[2048,128]{1,0:T(8,128)(2,1)S(1)} %bitcast.25), channel_id=1, source_target_pairs={{0,2},{1,3},{2,0},{3,1},{4,6},{5,7},{6,4},{7,5},{8,10},{9,11},{10,... | collective-permute-start | bytes 1572872 | tf_op jit(solution)/shard_map/ppermute | solution.py:56
  7.8 23.8 %collective-permute-start.1 = (bf16[2048,128]{1,0:T(8,128)(2,1)S(1)}, bf16[2048,128]{1,0:T(8,128)(2,1)S(1)}, u32[]{:S(2)}, u32[]{:S(2)}) collective-permute-start(bf16[2048,128]{1,0:T(8,128)(2,1)S(1)} %bitcast.26), channel_id=1, source_target_pairs={{0,3},{1,0},{2,1},{3,2},{4,7},{5,4},{6,5},{7,6},{8,9},{9,10},{10,1... | collective-permute-start | bytes 1572872 | tf_op jit(solution)/shard_map/ppermute | solution.py:56
  8.1 23.5 %collective-permute-start = (bf16[2048,128]{1,0:T(8,128)(2,1)S(1)}, bf16[2048,128]{1,0:T(8,128)(2,1)S(1)}, u32[]{:S(2)}, u32[]{:S(2)}) collective-permute-start(bf16[2048,128]{1,0:T(8,128)(2,1)S(1)} %bitcast.27), channel_id=1, source_target_pairs={{0,1},{1,2},{2,3},{3,0},{4,5},{5,6},{6,7},{7,4},{8,11},{9,8},{10,9... | collective-permute-start | bytes 1572872 | tf_op jit(solution)/shard_map/ppermute | solution.py:56
  16.7 26.2 %collective-permute-start.5 = (bf16[2048,128]{1,0:T(8,128)(2,1)S(1)}, bf16[2048,128]{1,0:T(8,128)(2,1)S(1)}, u32[]{:S(2)}, u32[]{:S(2)}) collective-permute-start(bf16[2048,128]{1,0:T(8,128)(2,1)S(1)} %collective-permute-done.3.refs_4_), channel_id=1, source_target_pairs={{0,3},{1,0},{2,1},{3,2},{4,7},{5,4},{6,5},{7,6},{8,9},{9,10},{10,1... | collective-permute-start | bytes 1572872 | tf_op jit(solution)/shard_map/ppermute | solution.py:56
  17.8 25.2 %collective-permute-start.4 = (bf16[2048,128]{1,0:T(8,128)(2,1)S(1)}, bf16[2048,128]{1,0:T(8,128)(2,1)S(1)}, u32[]{:S(2)}, u32[]{:S(2)}) collective-permute-start(bf16[2048,128]{1,0:T(8,128)(2,1)S(1)} %collective-permute-done.3.refs_4_), channel_id=1, source_target_pairs={{0,1},{1,2},{2,3},{3,0},{4,5},{5,6},{6,7},{7,4},{8,11},{9,8},{10,9... | collective-permute-start | bytes 1572872 | tf_op jit(solution)/shard_map/ppermute | solution.py:56
  19.4 23.6 %collective-permute-start.6 = (bf16[2048,128]{1,0:T(8,128)(2,1)S(1)}, bf16[2048,128]{1,0:T(8,128)(2,1)S(1)}, u32[]{:S(2)}, u32[]{:S(2)}) collective-permute-start(bf16[2048,128]{1,0:T(8,128)(2,1)S(1)} %collective-permute-done.2.refs_3_), channel_id=1, source_target_pairs={{0,4},{1,5},{2,6},{3,7},{4,0},{5,1},{6,2},{7,3},{8,12},{9,13},{10,... | collective-permute-start | bytes 1572872 | tf_op jit(solution)/shard_map/ppermute | solution.py:56
  31.6 22.6 %collective-permute-start.8 = (bf16[2048,128]{1,0:T(8,128)(2,1)S(1)}, bf16[2048,128]{1,0:T(8,128)(2,1)S(1)}, u32[]{:S(2)}, u32[]{:S(2)}) collective-permute-start(bf16[2048,128]{1,0:T(8,128)(2,1)S(1)} %bitcast.20), channel_id=1, source_target_pairs={{0,3},{1,0},{2,1},{3,2},{4,7},{5,4},{6,5},{7,6},{8,9},{9,10},{10,1... | collective-permute-start | bytes 1572872 | tf_op jit(solution)/shard_map/ppermute | solution.py:56
  31.6 22.6 %collective-permute-start.7 = (bf16[2048,128]{1,0:T(8,128)(2,1)S(1)}, bf16[2048,128]{1,0:T(8,128)(2,1)S(1)}, u32[]{:S(2)}, u32[]{:S(2)}) collective-permute-start(bf16[2048,128]{1,0:T(8,128)(2,1)S(1)} %bitcast.21), channel_id=1, source_target_pairs={{0,1},{1,2},{2,3},{3,0},{4,5},{5,6},{6,7},{7,4},{8,11},{9,8},{10,9... | collective-permute-start | bytes 1572872 | tf_op jit(solution)/shard_map/ppermute | solution.py:56
  57.2 22.5 %collective-permute-start.17 = (bf16[2048,128]{1,0:T(8,128)(2,1)S(1)}, bf16[2048,128]{1,0:T(8,128)(2,1)S(1)}, u32[]{:S(2)}, u32[]{:S(2)}) collective-permute-start(bf16[2048,128]{1,0:T(8,128)(2,1)S(1)} %collective-permute-done.9.refs_4_), channel_id=1, source_target_pairs={{0,3},{1,0},{2,1},{3,2},{4,7},{5,4},{6,5},{7,6},{8,9},{9,10},{10,1... | collective-permute-start | bytes 1572872 | tf_op jit(solution)/shard_map/ppermute | solution.py:56
  58.7 18.1 %collective-permute-start.16 = (bf16[2048,128]{1,0:T(8,128)(2,1)S(1)}, bf16[2048,128]{1,0:T(8,128)(2,1)S(1)}, u32[]{:S(2)}, u32[]{:S(2)}) collective-permute-start(bf16[2048,128]{1,0:T(8,128)(2,1)S(1)} %collective-permute-done.9.refs_4_), channel_id=1, source_target_pairs={{0,1},{1,2},{2,3},{3,0},{4,5},{5,6},{6,7},{7,4},{8,11},{9,8},{10,9... | collective-permute-start | bytes 1572872 | tf_op jit(solution)/shard_map/ppermute | solution.py:56
  62.2 17.5 %collective-permute-start.11 = (bf16[2,256,512]{2,1,0:T(8,128)(2,1)S(1)}, bf16[2,256,512]{2,1,0:T(8,128)(2,1)S(1)}, u32[]{:S(2)}, u32[]{:S(2)}) collective-permute-start(bf16[2,256,512]{2,1,0:T(8,128)(2,1)S(1)} %get-tuple-element.47), channel_id=1, source_target_pairs={{0,32},{1,33},{2,34},{3,35},{4,36},{5,37},{6,38},{7,39},{8,104},{9... | collective-permute-start | bytes 1572872 | tf_op jit(solution)/shard_map/ppermute | solution.py:56
  65.0 14.7 %collective-permute-start.12 = (bf16[2,256,512]{2,1,0:T(8,128)(2,1)S(1)}, bf16[2,256,512]{2,1,0:T(8,128)(2,1)S(1)}, u32[]{:S(2)}, u32[]{:S(2)}) collective-permute-start(bf16[2,256,512]{2,1,0:T(8,128)(2,1)S(1)} %get-tuple-element.48), channel_id=1, source_target_pairs={{0,96},{1,97},{2,98},{3,99},{4,100},{5,101},{6,102},{7,103},{8,40}... | collective-permute-start | bytes 1572872 | tf_op jit(solution)/shard_map/ppermute | solution.py:56
  76.8 13.5 %collective-permute-start.13 = (bf16[2,256,512]{2,1,0:T(8,128)(2,1)S(1)}, bf16[2,256,512]{2,1,0:T(8,128)(2,1)S(1)}, u32[]{:S(2)}, u32[]{:S(2)}) collective-permute-start(bf16[2,256,512]{2,1,0:T(8,128)(2,1)S(1)} %get-tuple-element.49), channel_id=1, source_target_pairs={{0,64},{1,65},{2,66},{3,67},{4,68},{5,69},{6,70},{7,71},{8,72},{9,... | collective-permute-start | bytes 1572872 | tf_op jit(solution)/shard_map/ppermute | solution.py:56
  98.8 19.0 %collective-permute-start.20 = (bf16[256,512]{1,0:T(8,128)(2,1)S(1)}, bf16[256,512]{1,0:T(8,128)(2,1)S(1)}, u32[]{:S(2)}, u32[]{:S(2)}) collective-permute-start(bf16[256,512]{1,0:T(8,128)(2,1)S(1)} %bitcast.43), channel_id=1, source_target_pairs={{0,32},{1,33},{2,34},{3,35},{4,36},{5,37},{6,38},{7,39},{8,104},{9... | collective-permute-start | bytes 786440 | tf_op jit(solution)/shard_map/ppermute | solution.py:56
  101.6 22.6 %collective-permute-start.21 = (bf16[256,512]{1,0:T(8,128)(2,1)S(1)}, bf16[256,512]{1,0:T(8,128)(2,1)S(1)}, u32[]{:S(2)}, u32[]{:S(2)}) collective-permute-start(bf16[256,512]{1,0:T(8,128)(2,1)S(1)} %bitcast.42), channel_id=1, source_target_pairs={{0,96},{1,97},{2,98},{3,99},{4,100},{5,101},{6,102},{7,103},{8,40}... | collective-permute-start | bytes 786440 | tf_op jit(solution)/shard_map/ppermute | solution.py:56
  101.6 22.6 %collective-permute-start.22 = (bf16[256,512]{1,0:T(8,128)(2,1)S(1)}, bf16[256,512]{1,0:T(8,128)(2,1)S(1)}, u32[]{:S(2)}, u32[]{:S(2)}) collective-permute-start(bf16[256,512]{1,0:T(8,128)(2,1)S(1)} %bitcast.41), channel_id=1, source_target_pairs={{0,64},{1,65},{2,66},{3,67},{4,68},{5,69},{6,70},{7,71},{8,72},{9,... | collective-permute-start | bytes 786440 | tf_op jit(solution)/shard_map/ppermute | solution.py:56
  103.2 20.9 %collective-permute-start.23 = (bf16[256,512]{1,0:T(8,128)(2,1)S(1)}, bf16[256,512]{1,0:T(8,128)(2,1)S(1)}, u32[]{:S(2)}, u32[]{:S(2)}) collective-permute-start(bf16[256,512]{1,0:T(8,128)(2,1)S(1)} %bitcast.40), channel_id=1, source_target_pairs={{0,16},{1,17},{2,18},{3,19},{4,20},{5,21},{6,22},{7,23},{8,24},{9,... | collective-permute-start | bytes 786440 | tf_op jit(solution)/shard_map/ppermute | solution.py:56
  106.3 18.3 %collective-permute-start.24 = (bf16[256,512]{1,0:T(8,128)(2,1)S(1)}, bf16[256,512]{1,0:T(8,128)(2,1)S(1)}, u32[]{:S(2)}, u32[]{:S(2)}) collective-permute-start(bf16[256,512]{1,0:T(8,128)(2,1)S(1)} %bitcast.39), channel_id=1, source_target_pairs={{0,80},{1,81},{2,82},{3,83},{4,84},{5,85},{6,86},{7,87},{8,88},{9,... | collective-permute-start | bytes 786440 | tf_op jit(solution)/shard_map/ppermute | solution.py:56
  117.8 13.5 %collective-permute-start.25 = (bf16[256,512]{1,0:T(8,128)(2,1)S(1)}, bf16[256,512]{1,0:T(8,128)(2,1)S(1)}, u32[]{:S(2)}, u32[]{:S(2)}) collective-permute-start(bf16[256,512]{1,0:T(8,128)(2,1)S(1)} %bitcast.38), channel_id=1, source_target_pairs={{0,48},{1,49},{2,50},{3,51},{4,52},{5,53},{6,54},{7,55},{8,120},{9... | collective-permute-start | bytes 786440 | tf_op jit(solution)/shard_map/ppermute | solution.py:56
  138.2 14.8 %collective-permute-start.33 = (bf16[512,512]{1,0:T(8,128)(2,1)S(1)}, bf16[512,512]{1,0:T(8,128)(2,1)S(1)}, u32[]{:S(2)}, u32[]{:S(2)}) collective-permute-start(bf16[512,512]{1,0:T(8,128)(2,1)S(1)} %get-tuple-element.68.refs_0_), channel_id=1, source_target_pairs={{0,96},{1,97},{2,98},{3,99},{4,100},{5,101},{6,102},{7,103},{8,40}... | collective-permute-start | bytes 1572872 | tf_op jit(solution)/shard_map/ppermute | solution.py:56
  139.3 15.3 %collective-permute-start.27 = (bf16[512,512]{1,0:T(8,128)(2,1)S(1)}, bf16[512,512]{1,0:T(8,128)(2,1)S(1)}, u32[]{:S(2)}, u32[]{:S(2)}) collective-permute-start(bf16[512,512]{1,0:T(8,128)(2,1)S(1)} %get-tuple-element.68.refs_0_), channel_id=1, source_target_pairs={{0,16},{1,17},{2,18},{3,19},{4,20},{5,21},{6,22},{7,23},{8,24},{9,... | collective-permute-start | bytes 1572872 | tf_op jit(solution)/shard_map/ppermute | solution.py:56
  159.2 16.0 %collective-permute-start.36 = (bf16[512,512]{1,0:T(8,128)(2,1)S(1)}, bf16[512,512]{1,0:T(8,128)(2,1)S(1)}, u32[]{:S(2)}, u32[]{:S(2)}) collective-permute-start(bf16[512,512]{1,0:T(8,128)(2,1)S(1)} %collective-permute-done.27.refs_6_), channel_id=1, source_target_pairs={{0,96},{1,97},{2,98},{3,99},{4,100},{5,101},{6,102},{7,103},{8,40}... | collective-permute-start | bytes 1572872 | tf_op jit(solution)/shard_map/ppermute | solution.py:56
  159.2 16.0 %collective-permute-start.31 = (bf16[512,512]{1,0:T(8,128)(2,1)S(1)}, bf16[512,512]{1,0:T(8,128)(2,1)S(1)}, u32[]{:S(2)}, u32[]{:S(2)}) collective-permute-start(bf16[512,512]{1,0:T(8,128)(2,1)S(1)} %collective-permute-done.27.refs_6_), channel_id=1, source_target_pairs={{0,32},{1,33},{2,34},{3,35},{4,36},{5,37},{6,38},{7,39},{8,104},{9... | collective-permute-start | bytes 1572872 | tf_op jit(solution)/shard_map/ppermute | solution.py:56
  (23 other events, 291.9 us)

commit v4 on v3

--- a/solution.py
+++ b/solution.py
@@ -297,9 +297,9 @@
         )
         at += rows
         first += count
-    grad = split(grad_ref[...])
-    right = mm3(grad, split(roots_ref[1]))
-    update_ref[...] = mm3(split(roots_ref[0]), split(right)).astype(jnp.bfloat16)
+    left, right = roots_ref[0].astype(jnp.bfloat16), roots_ref[1].astype(jnp.bfloat16)
+    half = mm(grad_ref[...].astype(jnp.bfloat16), right, ((1,), (0,)))
+    update_ref[...] = mm(left, half.astype(jnp.bfloat16), ((1,), (0,))).astype(jnp.bfloat16)
 
 
 def apply_roots(terms, roots):

time: 184 us -> 183 us (level)
  Pallas kernels: 39.3 us -> 32.5 us
  starting transfers between devices: 62.4 us -> 65.8 us
  waiting for transfers between devices: 78.8 us -> 81.2 us
    pallas_call x1, Pallas kernels: 7.61 us -> 2.02 us  [roots_of(): pl.pallas_call(roots_kernel, out_shape=jax.ShapeDtypeStruct(stats.shape,...]
    ppermute x42, starting transfers between devices: 62.4 us -> 65.8 us  [move(): return lax.ppermute(value, ('dp', 'mp'), route)]
    ppermute x42, waiting for transfers between devices: 78.8 us -> 81.2 us  [move(): return lax.ppermute(value, ('dp', 'mp'), route)]
  transfers between devices with their start and end apart: 42 -> 42, of which waited for: 18 -> 19; matrix products, arithmetic and copies ran while one was open for 0% -> 0% of each run, Pallas kernels for 19% -> 16%
where the time goes in v4:
time: 183 us
  waiting for transfers between devices  81.2 us (44%)
  starting transfers between devices  65.8 us (36%)
  Pallas kernels  32.5 us (18%)
  local copies, waits for them, and re-layouts  1.85 us (1%)
    ppermute x42, waiting for transfers between devices, move(): return lax.ppermute(value, ('dp', 'mp'), route)  81.2 us
    ppermute x42, starting transfers between devices, move(): return lax.ppermute(value, ('dp', 'mp'), route)  65.8 us
    pallas_call x2, Pallas kernels, grad_chunk(): pl.pallas_call(functools.partial(grad_kernel, rows, span), out_shape=(hal...  17.5 us
    pallas_call x2, Pallas kernels, place(): pl.pallas_call(functools.partial(place_kernel, whence, int(aliased)), out...  6.02 us
  transfers between devices with their start and end apart: 42, of which 19 were waited for; matrix products, arithmetic and copies ran while one was open for 0% of the time, Pallas kernels for 16%

profile of v4, /device:TPU:1, one launch (start us, length us, event | category | flops | bytes accessed | tf_op | source)
XLA Modules:
  0.0 183.0 jit_solution(8204208112218659391)
XLA Ops:
  10.5 6.2 %collective-permute-done.3.refs_4_ = bf16[2048,128]{1,0:T(8,128)(2,1)S(1)} collective-permute-done((bf16[2048,128]{1,0:T(8,128)(2,1)S(1)}, bf16[2048,128]{1,0:T(8,128)(2,1)S(1)}, u32[]{:S(2)}, u32[]{:S(2)}) %collective-permute-start.3) | collective-permute-done | bytes 524320 | tf_op jit(solution)/shard_map/ppermute | solution.py:56
  20.5 11.1 %collective-permute-done.1.refs_2_ = bf16[2048,128]{1,0:T(8,128)(2,1)S(1)} collective-permute-done((bf16[2048,128]{1,0:T(8,128)(2,1)S(1)}, bf16[2048,128]{1,0:T(8,128)(2,1)S(1)}, u32[]{:S(2)}, u32[]{:S(2)}) %collective-permute-start.1) | collective-permute-done | bytes 524320 | tf_op jit(solution)/shard_map/ppermute | solution.py:56
  34.3 8.6 %collective-permute-done.5.refs_6_ = bf16[2048,128]{1,0:T(8,128)(2,1)S(1)} collective-permute-done((bf16[2048,128]{1,0:T(8,128)(2,1)S(1)}, bf16[2048,128]{1,0:T(8,128)(2,1)S(1)}, u32[]{:S(2)}, u32[]{:S(2)}) %collective-permute-start.5) | collective-permute-done | bytes 524320 | tf_op jit(solution)/shard_map/ppermute | solution.py:56
  43.0 8.8 %grad_chunk.2 = (bf16[8,256,512]{2,1,0:T(8,128)(2,1)S(1)}, bf16[8,256,512]{2,1,0:T(8,128)(2,1)S(1)}) custom-call(s32[16]{0:T(128)S(1)} %bitcast.29, bf16[2048,128]{1,0:T(8,128)(2,1)S(1)} %bitcast.28, bf16[2048,128]{1,0:T(8,128)(2,1)S(1)} %collective-permute-done.refs_1_, bf16[2048,128]{1,0:T(8,128)(2,1)S(1)} %collective-permute-done.1.refs_2_, ...), custom_call_target="tpu_custom_call" | custom-call | flops 9813332992 | bytes 1024 | tf_op jit(solution)/shard_map/grad_chunk/pallas_call | solution.py:171
  54.2 3.0 %collective-permute-start.10 = (bf16[8,256,512]{2,1,0:T(8,128)(2,1)S(1)}, bf16[8,256,512]{2,1,0:T(8,128)(2,1)S(1)}, u32[]{:S(2)}, u32[]{:S(2)}) collective-permute-start(bf16[8,256,512]{2,1,0:T(8,128)(2,1)S(1)} %get-tuple-element.45), channel_id=1, source_target_pairs={{0,8},{1,9},{2,10},{3,11},{4,12},{5,13},{6,14},{7,15},{8,0},{9,1},... | collective-permute-start | bytes 6291464 | tf_op jit(solution)/shard_map/ppermute | solution.py:56
  62.2 2.8 %collective-permute-start.11 = (bf16[2,256,512]{2,1,0:T(8,128)(2,1)S(1)}, bf16[2,256,512]{2,1,0:T(8,128)(2,1)S(1)}, u32[]{:S(2)}, u32[]{:S(2)}) collective-permute-start(bf16[2,256,512]{2,1,0:T(8,128)(2,1)S(1)} %get-tuple-element.47), channel_id=1, source_target_pairs={{0,32},{1,33},{2,34},{3,35},{4,36},{5,37},{6,38},{7,39},{8,104},{9... | collective-permute-start | bytes 1572872 | tf_op jit(solution)/shard_map/ppermute | solution.py:56
  65.0 5.4 %collective-permute-done.15.refs_3_ = bf16[2048,128]{1,0:T(8,128)(2,1)S(1)} collective-permute-done((bf16[2048,128]{1,0:T(8,128)(2,1)S(1)}, bf16[2048,128]{1,0:T(8,128)(2,1)S(1)}, u32[]{:S(2)}, u32[]{:S(2)}) %collective-permute-start.15) | collective-permute-done | bytes 524320 | tf_op jit(solution)/shard_map/ppermute | solution.py:56
  70.4 6.4 %collective-permute-done.16.refs_5_ = bf16[2048,128]{1,0:T(8,128)(2,1)S(1)} collective-permute-done((bf16[2048,128]{1,0:T(8,128)(2,1)S(1)}, bf16[2048,128]{1,0:T(8,128)(2,1)S(1)}, u32[]{:S(2)}, u32[]{:S(2)}) %collective-permute-start.16) | collective-permute-done | bytes 524320 | tf_op jit(solution)/shard_map/ppermute | solution.py:56
  76.8 2.9 %collective-permute-start.13 = (bf16[2,256,512]{2,1,0:T(8,128)(2,1)S(1)}, bf16[2,256,512]{2,1,0:T(8,128)(2,1)S(1)}, u32[]{:S(2)}, u32[]{:S(2)}) collective-permute-start(bf16[2,256,512]{2,1,0:T(8,128)(2,1)S(1)} %get-tuple-element.49), channel_id=1, source_target_pairs={{0,64},{1,65},{2,66},{3,67},{4,68},{5,69},{6,70},{7,71},{8,72},{9,... | collective-permute-start | bytes 1572872 | tf_op jit(solution)/shard_map/ppermute | solution.py:56
  81.5 8.8 %grad_chunk.3 = (bf16[8,256,512]{2,1,0:T(8,128)(2,1)S(1)}, bf16[8,256,512]{2,1,0:T(8,128)(2,1)S(1)}) custom-call(s32[16]{0:T(128)S(1)} %bitcast.30, bf16[2048,128]{1,0:T(8,128)(2,1)S(1)} %bitcast.23, bf16[2048,128]{1,0:T(8,128)(2,1)S(1)} %collective-permute-done.7.refs_1_, bf16[2048,128]{1,0:T(8,128)(2,1)S(1)} %collective-permute-done.8.refs_2_, ...), custom_call_target="tpu_custom_call" | custom-call | flops 9813332992 | bytes 1024 | tf_op jit(solution)/shard_map/grad_chunk/pallas_call | solution.py:171
  90.2 3.4 %collective-permute-start.19 = (bf16[8,256,512]{2,1,0:T(8,128)(2,1)S(1)}, bf16[8,256,512]{2,1,0:T(8,128)(2,1)S(1)}, u32[]{:S(2)}, u32[]{:S(2)}) collective-permute-start(bf16[8,256,512]{2,1,0:T(8,128)(2,1)S(1)} %get-tuple-element.58), channel_id=1, source_target_pairs={{0,8},{1,9},{2,10},{3,11},{4,12},{5,13},{6,14},{7,15},{8,0},{9,1},... | collective-permute-start | bytes 6291464 | tf_op jit(solution)/shard_map/ppermute | solution.py:56
  94.2 3.4 %collective-permute-start.14 = (bf16[256,512]{1,0:T(8,128)(2,1)S(1)}, bf16[256,512]{1,0:T(8,128)(2,1)S(1)}, u32[]{:S(2)}, u32[]{:S(2)}) collective-permute-start(bf16[256,512]{1,0:T(8,128)(2,1)S(1)} %get-tuple-element.51), channel_id=1, source_target_pairs={{0,16},{1,17},{2,18},{3,19},{4,20},{5,21},{6,22},{7,23},{8,24},{9,... | collective-permute-start | bytes 786440 | tf_op jit(solution)/shard_map/ppermute | solution.py:56
  103.2 3.1 %collective-permute-start.23 = (bf16[256,512]{1,0:T(8,128)(2,1)S(1)}, bf16[256,512]{1,0:T(8,128)(2,1)S(1)}, u32[]{:S(2)}, u32[]{:S(2)}) collective-permute-start(bf16[256,512]{1,0:T(8,128)(2,1)S(1)} %bitcast.40), channel_id=1, source_target_pairs={{0,16},{1,17},{2,18},{3,19},{4,20},{5,21},{6,22},{7,23},{8,24},{9,... | collective-permute-start | bytes 786440 | tf_op jit(solution)/shard_map/ppermute | solution.py:56
  106.3 3.2 %collective-permute-start.24 = (bf16[256,512]{1,0:T(8,128)(2,1)S(1)}, bf16[256,512]{1,0:T(8,128)(2,1)S(1)}, u32[]{:S(2)}, u32[]{:S(2)}) collective-permute-start(bf16[256,512]{1,0:T(8,128)(2,1)S(1)} %bitcast.39), channel_id=1, source_target_pairs={{0,80},{1,81},{2,82},{3,83},{4,84},{5,85},{6,86},{7,87},{8,88},{9,... | collective-permute-start | bytes 786440 | tf_op jit(solution)/shard_map/ppermute | solution.py:56
  109.6 8.2 %collective-permute-done.20.refs_3_ = bf16[256,512]{1,0:T(8,128)(2,1)S(1)} collective-permute-done((bf16[256,512]{1,0:T(8,128)(2,1)S(1)}, bf16[256,512]{1,0:T(8,128)(2,1)S(1)}, u32[]{:S(2)}, u32[]{:S(2)}) %collective-permute-start.20) | collective-permute-done | bytes 262176 | tf_op jit(solution)/shard_map/ppermute | solution.py:56
  117.8 6.3 %collective-permute-start.25 = (bf16[256,512]{1,0:T(8,128)(2,1)S(1)}, bf16[256,512]{1,0:T(8,128)(2,1)S(1)}, u32[]{:S(2)}, u32[]{:S(2)}) collective-permute-start(bf16[256,512]{1,0:T(8,128)(2,1)S(1)} %bitcast.38), channel_id=1, source_target_pairs={{0,48},{1,49},{2,50},{3,51},{4,52},{5,53},{6,54},{7,55},{8,120},{9... | collective-permute-start | bytes 786440 | tf_op jit(solution)/shard_map/ppermute | solution.py:56
  124.7 6.6 %collective-permute-done.25.refs_8_ = bf16[256,512]{1,0:T(8,128)(2,1)S(1)} collective-permute-done((bf16[256,512]{1,0:T(8,128)(2,1)S(1)}, bf16[256,512]{1,0:T(8,128)(2,1)S(1)}, u32[]{:S(2)}, u32[]{:S(2)}) %collective-permute-start.25) | collective-permute-done | bytes 262176 | tf_op jit(solution)/shard_map/ppermute | solution.py:56
  131.2 3.8 %collective-permute-done.26.refs_9_ = bf16[256,512]{1,0:T(8,128)(2,1)S(1)} collective-permute-done((bf16[256,512]{1,0:T(8,128)(2,1)S(1)}, bf16[256,512]{1,0:T(8,128)(2,1)S(1)}, u32[]{:S(2)}, u32[]{:S(2)}) %collective-permute-start.26) | collective-permute-done | bytes 262176 | tf_op jit(solution)/shard_map/ppermute | solution.py:56
  139.3 3.2 %statistics.1.stats_ref = f32[2,512,512]{2,1,0:T(8,128)} custom-call(f32[512,512]{1,0:T(8,128)S(1)} %get-tuple-element.69.grad_ref, f32[2,512,512]{2,1,0:T(8,128)S(1)} %bitcast.34), custom_call_target="tpu_custom_call" | custom-call | flops 3680000000 | bytes 1024 | tf_op jit(solution)/shard_map/statistics/pallas_call | solution.py:328
  142.4 7.5 %collective-permute-done.28.refs_2_ = bf16[512,512]{1,0:T(8,128)(2,1)S(1)} collective-permute-done((bf16[512,512]{1,0:T(8,128)(2,1)S(1)}, bf16[512,512]{1,0:T(8,128)(2,1)S(1)}, u32[]{:S(2)}, u32[]{:S(2)}) %collective-permute-start.28) | collective-permute-done | bytes 524320 | tf_op jit(solution)/shard_map/ppermute | solution.py:56
  153.3 4.9 %collective-permute-done.30.refs_7_ = bf16[512,512]{1,0:T(8,128)(2,1)S(1)} collective-permute-done((bf16[512,512]{1,0:T(8,128)(2,1)S(1)}, bf16[512,512]{1,0:T(8,128)(2,1)S(1)}, u32[]{:S(2)}, u32[]{:S(2)}) %collective-permute-start.30) | collective-permute-done | bytes 524320 | tf_op jit(solution)/shard_map/ppermute | solution.py:56
  163.1 3.0 %place.2.refs_8_ = bf16[4096,1024]{1,0:T(8,128)(2,1)} custom-call(s32[16]{0:T(128)S(1)} %bitcast.31, bf16[512,512]{1,0:T(8,128)(2,1)S(1)} %get-tuple-element.68.refs_0_, bf16[512,512]{1,0:T(8,128)(2,1)S(1)} %collective-permute-done.29.refs_1_, bf16[512,512]{1,0:T(8,128)(2,1)S(1)} %collective-permute-done.28.refs_2_, ...), custom_call_target="tpu_custom_call" | custom-call | flops 4255000064 | bytes 1024 | tf_op jit(solution)/shard_map/place/pallas_call | solution.py:417
  172.3 4.5 %collective-permute-start.35 = (bf16[512,512]{1,0:T(8,128)(2,1)S(1)}, bf16[512,512]{1,0:T(8,128)(2,1)S(1)}, u32[]{:S(2)}, u32[]{:S(2)}) collective-permute-start(bf16[512,512]{1,0:T(8,128)(2,1)S(1)} %collective-permute-done.31.refs_0_), channel_id=1, source_target_pairs={{0,8},{1,9},{2,10},{3,11},{4,12},{5,13},{6,14},{7,15},{8,0},{9,1},... | collective-permute-start | bytes 1572872 | tf_op jit(solution)/shard_map/ppermute | solution.py:56
  179.8 3.0 %place.3 = bf16[4096,1024]{1,0:T(8,128)(2,1)} custom-call(s32[16]{0:T(128)S(1)} %bitcast.33, bf16[512,512]{1,0:T(8,128)(2,1)S(1)} %collective-permute-done.31.refs_0_, bf16[512,512]{1,0:T(8,128)(2,1)S(1)} %collective-permute-done.35.refs_1_, bf16[512,512]{1,0:T(8,128)(2,1)S(1)} %collective-permute-done.36.refs_2_, ...), custom_call_target="tpu_custom_call", output_to_operand_aliasing={{}: (9, {})} | custom-call | flops 4255000064 | bytes 1024 | tf_op jit(solution)/shard_map/place/pallas_call | solution.py:417
  (82 shorter events, 53.4 us)
Async XLA Ops:
  2.5 14.2 %collective-permute-start.3 = (bf16[2048,128]{1,0:T(8,128)(2,1)S(1)}, bf16[2048,128]{1,0:T(8,128)(2,1)S(1)}, u32[]{:S(2)}, u32[]{:S(2)}) collective-permute-start(bf16[2048,128]{1,0:T(8,128)(2,1)S(1)} %bitcast.24), channel_id=1, source_target_pairs={{0,4},{1,5},{2,6},{3,7},{4,0},{5,1},{6,2},{7,3},{8,12},{9,13},{10,... | collective-permute-start | bytes 1572872 | tf_op jit(solution)/shard_map/ppermute | solution.py:56
  5.0 14.3 %collective-permute-start.2 = (bf16[2048,128]{1,0:T(8,128)(2,1)S(1)}, bf16[2048,128]{1,0:T(8,128)(2,1)S(1)}, u32[]{:S(2)}, u32[]{:S(2)}) collective-permute-start(bf16[2048,128]{1,0:T(8,128)(2,1)S(1)} %bitcast.25), channel_id=1, source_target_pairs={{0,2},{1,3},{2,0},{3,1},{4,6},{5,7},{6,4},{7,5},{8,10},{9,11},{10,... | collective-permute-start | bytes 1572872 | tf_op jit(solution)/shard_map/ppermute | solution.py:56
  7.8 23.8 %collective-permute-start.1 = (bf16[2048,128]{1,0:T(8,128)(2,1)S(1)}, bf16[2048,128]{1,0:T(8,128)(2,1)S(1)}, u32[]{:S(2)}, u32[]{:S(2)}) collective-permute-start(bf16[2048,128]{1,0:T(8,128)(2,1)S(1)} %bitcast.26), channel_id=1, source_target_pairs={{0,3},{1,0},{2,1},{3,2},{4,7},{5,4},{6,5},{7,6},{8,9},{9,10},{10,1... | collective-permute-start | bytes 1572872 | tf_op jit(solution)/shard_map/ppermute | solution.py:56
  8.1 23.5 %collective-permute-start = (bf16[2048,128]{1,0:T(8,128)(2,1)S(1)}, bf16[2048,128]{1,0:T(8,128)(2,1)S(1)}, u32[]{:S(2)}, u32[]{:S(2)}) collective-permute-start(bf16[2048,128]{1,0:T(8,128)(2,1)S(1)} %bitcast.27), channel_id=1, source_target_pairs={{0,1},{1,2},{2,3},{3,0},{4,5},{5,6},{6,7},{7,4},{8,11},{9,8},{10,9... | collective-permute-start | bytes 1572872 | tf_op jit(solution)/shard_map/ppermute | solution.py:56
  16.7 26.2 %collective-permute-start.5 = (bf16[2048,128]{1,0:T(8,128)(2,1)S(1)}, bf16[2048,128]{1,0:T(8,128)(2,1)S(1)}, u32[]{:S(2)}, u32[]{:S(2)}) collective-permute-start(bf16[2048,128]{1,0:T(8,128)(2,1)S(1)} %collective-permute-done.3.refs_4_), channel_id=1, source_target_pairs={{0,3},{1,0},{2,1},{3,2},{4,7},{5,4},{6,5},{7,6},{8,9},{9,10},{10,1... | collective-permute-start | bytes 1572872 | tf_op jit(solution)/shard_map/ppermute | solution.py:56
  17.8 25.2 %collective-permute-start.4 = (bf16[2048,128]{1,0:T(8,128)(2,1)S(1)}, bf16[2048,128]{1,0:T(8,128)(2,1)S(1)}, u32[]{:S(2)}, u32[]{:S(2)}) collective-permute-start(bf16[2048,128]{1,0:T(8,128)(2,1)S(1)} %collective-permute-done.3.refs_4_), channel_id=1, source_target_pairs={{0,1},{1,2},{2,3},{3,0},{4,5},{5,6},{6,7},{7,4},{8,11},{9,8},{10,9... | collective-permute-start | bytes 1572872 | tf_op jit(solution)/shard_map/ppermute | solution.py:56
  19.4 23.6 %collective-permute-start.6 = (bf16[2048,128]{1,0:T(8,128)(2,1)S(1)}, bf16[2048,128]{1,0:T(8,128)(2,1)S(1)}, u32[]{:S(2)}, u32[]{:S(2)}) collective-permute-start(bf16[2048,128]{1,0:T(8,128)(2,1)S(1)} %collective-permute-done.2.refs_3_), channel_id=1, source_target_pairs={{0,4},{1,5},{2,6},{3,7},{4,0},{5,1},{6,2},{7,3},{8,12},{9,13},{10,... | collective-permute-start | bytes 1572872 | tf_op jit(solution)/shard_map/ppermute | solution.py:56
  31.6 22.6 %collective-permute-start.8 = (bf16[2048,128]{1,0:T(8,128)(2,1)S(1)}, bf16[2048,128]{1,0:T(8,128)(2,1)S(1)}, u32[]{:S(2)}, u32[]{:S(2)}) collective-permute-start(bf16[2048,128]{1,0:T(8,128)(2,1)S(1)} %bitcast.20), channel_id=1, source_target_pairs={{0,3},{1,0},{2,1},{3,2},{4,7},{5,4},{6,5},{7,6},{8,9},{9,10},{10,1... | collective-permute-start | bytes 1572872 | tf_op jit(solution)/shard_map/ppermute | solution.py:56
  31.6 22.6 %collective-permute-start.7 = (bf16[2048,128]{1,0:T(8,128)(2,1)S(1)}, bf16[2048,128]{1,0:T(8,128)(2,1)S(1)}, u32[]{:S(2)}, u32[]{:S(2)}) collective-permute-start(bf16[2048,128]{1,0:T(8,128)(2,1)S(1)} %bitcast.21), channel_id=1, source_target_pairs={{0,1},{1,2},{2,3},{3,0},{4,5},{5,6},{6,7},{7,4},{8,11},{9,8},{10,9... | collective-permute-start | bytes 1572872 | tf_op jit(solution)/shard_map/ppermute | solution.py:56
  57.2 22.5 %collective-permute-start.17 = (bf16[2048,128]{1,0:T(8,128)(2,1)S(1)}, bf16[2048,128]{1,0:T(8,128)(2,1)S(1)}, u32[]{:S(2)}, u32[]{:S(2)}) collective-permute-start(bf16[2048,128]{1,0:T(8,128)(2,1)S(1)} %collective-permute-done.9.refs_4_), channel_id=1, source_target_pairs={{0,3},{1,0},{2,1},{3,2},{4,7},{5,4},{6,5},{7,6},{8,9},{9,10},{10,1... | collective-permute-start | bytes 1572872 | tf_op jit(solution)/shard_map/ppermute | solution.py:56
  58.7 18.1 %collective-permute-start.16 = (bf16[2048,128]{1,0:T(8,128)(2,1)S(1)}, bf16[2048,128]{1,0:T(8,128)(2,1)S(1)}, u32[]{:S(2)}, u32[]{:S(2)}) collective-permute-start(bf16[2048,128]{1,0:T(8,128)(2,1)S(1)} %collective-permute-done.9.refs_4_), channel_id=1, source_target_pairs={{0,1},{1,2},{2,3},{3,0},{4,5},{5,6},{6,7},{7,4},{8,11},{9,8},{10,9... | collective-permute-start | bytes 1572872 | tf_op jit(solution)/shard_map/ppermute | solution.py:56
  62.2 17.5 %collective-permute-start.11 = (bf16[2,256,512]{2,1,0:T(8,128)(2,1)S(1)}, bf16[2,256,512]{2,1,0:T(8,128)(2,1)S(1)}, u32[]{:S(2)}, u32[]{:S(2)}) collective-permute-start(bf16[2,256,512]{2,1,0:T(8,128)(2,1)S(1)} %get-tuple-element.47), channel_id=1, source_target_pairs={{0,32},{1,33},{2,34},{3,35},{4,36},{5,37},{6,38},{7,39},{8,104},{9... | collective-permute-start | bytes 1572872 | tf_op jit(solution)/shard_map/ppermute | solution.py:56
  65.0 14.7 %collective-permute-start.12 = (bf16[2,256,512]{2,1,0:T(8,128)(2,1)S(1)}, bf16[2,256,512]{2,1,0:T(8,128)(2,1)S(1)}, u32[]{:S(2)}, u32[]{:S(2)}) collective-permute-start(bf16[2,256,512]{2,1,0:T(8,128)(2,1)S(1)} %get-tuple-element.48), channel_id=1, source_target_pairs={{0,96},{1,97},{2,98},{3,99},{4,100},{5,101},{6,102},{7,103},{8,40}... | collective-permute-start | bytes 1572872 | tf_op jit(solution)/shard_map/ppermute | solution.py:56
  76.8 13.5 %collective-permute-start.13 = (bf16[2,256,512]{2,1,0:T(8,128)(2,1)S(1)}, bf16[2,256,512]{2,1,0:T(8,128)(2,1)S(1)}, u32[]{:S(2)}, u32[]{:S(2)}) collective-permute-start(bf16[2,256,512]{2,1,0:T(8,128)(2,1)S(1)} %get-tuple-element.49), channel_id=1, source_target_pairs={{0,64},{1,65},{2,66},{3,67},{4,68},{5,69},{6,70},{7,71},{8,72},{9,... | collective-permute-start | bytes 1572872 | tf_op jit(solution)/shard_map/ppermute | solution.py:56
  98.8 19.0 %collective-permute-start.20 = (bf16[256,512]{1,0:T(8,128)(2,1)S(1)}, bf16[256,512]{1,0:T(8,128)(2,1)S(1)}, u32[]{:S(2)}, u32[]{:S(2)}) collective-permute-start(bf16[256,512]{1,0:T(8,128)(2,1)S(1)} %bitcast.43), channel_id=1, source_target_pairs={{0,32},{1,33},{2,34},{3,35},{4,36},{5,37},{6,38},{7,39},{8,104},{9... | collective-permute-start | bytes 786440 | tf_op jit(solution)/shard_map/ppermute | solution.py:56
  101.6 22.6 %collective-permute-start.21 = (bf16[256,512]{1,0:T(8,128)(2,1)S(1)}, bf16[256,512]{1,0:T(8,128)(2,1)S(1)}, u32[]{:S(2)}, u32[]{:S(2)}) collective-permute-start(bf16[256,512]{1,0:T(8,128)(2,1)S(1)} %bitcast.42), channel_id=1, source_target_pairs={{0,96},{1,97},{2,98},{3,99},{4,100},{5,101},{6,102},{7,103},{8,40}... | collective-permute-start | bytes 786440 | tf_op jit(solution)/shard_map/ppermute | solution.py:56
  101.6 22.6 %collective-permute-start.22 = (bf16[256,512]{1,0:T(8,128)(2,1)S(1)}, bf16[256,512]{1,0:T(8,128)(2,1)S(1)}, u32[]{:S(2)}, u32[]{:S(2)}) collective-permute-start(bf16[256,512]{1,0:T(8,128)(2,1)S(1)} %bitcast.41), channel_id=1, source_target_pairs={{0,64},{1,65},{2,66},{3,67},{4,68},{5,69},{6,70},{7,71},{8,72},{9,... | collective-permute-start | bytes 786440 | tf_op jit(solution)/shard_map/ppermute | solution.py:56
  103.2 20.9 %collective-permute-start.23 = (bf16[256,512]{1,0:T(8,128)(2,1)S(1)}, bf16[256,512]{1,0:T(8,128)(2,1)S(1)}, u32[]{:S(2)}, u32[]{:S(2)}) collective-permute-start(bf16[256,512]{1,0:T(8,128)(2,1)S(1)} %bitcast.40), channel_id=1, source_target_pairs={{0,16},{1,17},{2,18},{3,19},{4,20},{5,21},{6,22},{7,23},{8,24},{9,... | collective-permute-start | bytes 786440 | tf_op jit(solution)/shard_map/ppermute | solution.py:56
  106.3 18.3 %collective-permute-start.24 = (bf16[256,512]{1,0:T(8,128)(2,1)S(1)}, bf16[256,512]{1,0:T(8,128)(2,1)S(1)}, u32[]{:S(2)}, u32[]{:S(2)}) collective-permute-start(bf16[256,512]{1,0:T(8,128)(2,1)S(1)} %bitcast.39), channel_id=1, source_target_pairs={{0,80},{1,81},{2,82},{3,83},{4,84},{5,85},{6,86},{7,87},{8,88},{9,... | collective-permute-start | bytes 786440 | tf_op jit(solution)/shard_map/ppermute | solution.py:56
  117.8 13.5 %collective-permute-start.25 = (bf16[256,512]{1,0:T(8,128)(2,1)S(1)}, bf16[256,512]{1,0:T(8,128)(2,1)S(1)}, u32[]{:S(2)}, u32[]{:S(2)}) collective-permute-start(bf16[256,512]{1,0:T(8,128)(2,1)S(1)} %bitcast.38), channel_id=1, source_target_pairs={{0,48},{1,49},{2,50},{3,51},{4,52},{5,53},{6,54},{7,55},{8,120},{9... | collective-permute-start | bytes 786440 | tf_op jit(solution)/shard_map/ppermute | solution.py:56
  137.0 15.1 %collective-permute-start.33 = (bf16[512,512]{1,0:T(8,128)(2,1)S(1)}, bf16[512,512]{1,0:T(8,128)(2,1)S(1)}, u32[]{:S(2)}, u32[]{:S(2)}) collective-permute-start(bf16[512,512]{1,0:T(8,128)(2,1)S(1)} %get-tuple-element.68.refs_0_), channel_id=1, source_target_pairs={{0,96},{1,97},{2,98},{3,99},{4,100},{5,101},{6,102},{7,103},{8,40}... | collective-permute-start | bytes 1572872 | tf_op jit(solution)/shard_map/ppermute | solution.py:56
  138.0 15.3 %collective-permute-start.27 = (bf16[512,512]{1,0:T(8,128)(2,1)S(1)}, bf16[512,512]{1,0:T(8,128)(2,1)S(1)}, u32[]{:S(2)}, u32[]{:S(2)}) collective-permute-start(bf16[512,512]{1,0:T(8,128)(2,1)S(1)} %get-tuple-element.68.refs_0_), channel_id=1, source_target_pairs={{0,16},{1,17},{2,18},{3,19},{4,20},{5,21},{6,22},{7,23},{8,24},{9,... | collective-permute-start | bytes 1572872 | tf_op jit(solution)/shard_map/ppermute | solution.py:56
  158.3 14.1 %collective-permute-start.36 = (bf16[512,512]{1,0:T(8,128)(2,1)S(1)}, bf16[512,512]{1,0:T(8,128)(2,1)S(1)}, u32[]{:S(2)}, u32[]{:S(2)}) collective-permute-start(bf16[512,512]{1,0:T(8,128)(2,1)S(1)} %collective-permute-done.27.refs_6_), channel_id=1, source_target_pairs={{0,96},{1,97},{2,98},{3,99},{4,100},{5,101},{6,102},{7,103},{8,40}... | collective-permute-start | bytes 1572872 | tf_op jit(solution)/shard_map/ppermute | solution.py:56
  158.3 14.1 %collective-permute-start.31 = (bf16[512,512]{1,0:T(8,128)(2,1)S(1)}, bf16[512,512]{1,0:T(8,128)(2,1)S(1)}, u32[]{:S(2)}, u32[]{:S(2)}) collective-permute-start(bf16[512,512]{1,0:T(8,128)(2,1)S(1)} %collective-permute-done.27.refs_6_), channel_id=1, source_target_pairs={{0,32},{1,33},{2,34},{3,35},{4,36},{5,37},{6,38},{7,39},{8,104},{9... | collective-permute-start | bytes 1572872 | tf_op jit(solution)/shard_map/ppermute | solution.py:56
  (23 other events, 300.5 us)
